TPU v7x, 32 devices: a whole 2x2x4 slice. The times are simulated.
32 devices in a mesh: dp: 4 (over y, x), chan: 8 (over z, core).
Axes of the slice: x: 2, y: 2, z: 4, core: 2. Of those that a mesh axis runs over, the one named last changes fastest.
Arguments:
- x_in: bfloat16 [4, 48, 360, 800], P('dp', None, None, 'chan'), may hold values from -12 to 12
- cotangent: bfloat16 [4, 48, 360, 800], P('dp', None, None, 'chan'), may hold values from -9 to 9
- land: int32 [4, 48, 360], P('dp'), may hold values 0 or 1
- grid_res: int32 [4], P('dp'), may hold values from 0 to 1
- dw_kernel: bfloat16 [49, 800], replicated, may hold values from -0.875 to 0.875
- gain: float32 [800], replicated, may hold values from 0.5 to 1.5
- shift: float32 [800], replicated, may hold values from -1.75 to 1.75
- res_bias: float32 [2, 800], replicated, may hold values from -3 to 3
- w_in: bfloat16 [800, 3200], replicated, may hold values from -0.21875 to 0.21875
- b_in: float32 [3200], replicated, may hold values from -1.75 to 1.75
- w_out: bfloat16 [3200, 800], replicated, may hold values from -0.109375 to 0.109375
- b_out: float32 [800], replicated, may hold values from -1.75 to 1.75
Outputs:
- mixed: bfloat16 [4, 48, 360, 800], P('dp', None, None, 'chan')
- x_grad: bfloat16 [4, 48, 360, 800], P('dp', None, None, 'chan')
- g_kernel: float32 [49, 800], replicated
- g_gain: float32 [800], replicated
- g_shift: float32 [800], replicated
- g_res_bias: float32 [2, 800], replicated
- g_w_in: float32 [800, 3200], replicated
- g_b_in: float32 [3200], replicated
- g_w_out: float32 [3200, 800], replicated
- g_b_out: float32 [800], replicated
All inputs are finite; a program needn't handle non-finite values. No bound on the sum of `land` on one device may be relied on, other than what follows from the above.
Results may differ from a plain program's by a relative error of at most 0.01.
Values may be sent and summed in bfloat16 or wider, within the bound.
No kernel may reach another device: no remote copies, remote signals or barrier semaphores. Data moves between devices by JAX's collectives and lax.ppermute only.
A program may use at most 320 MiB of HBM per device.

v0:
```python
from functools import partial
import math

import jax
import jax.numpy as jnp
from jax import lax
from jax.sharding import PartitionSpec as P


def padded_2(block, sides, width):
    for axis, dim in sides:
        count = lax.axis_size(axis)
        forward = [(i, i + 1) for i in range(count - 1)]
        backward = [(target, source) for source, target in forward]
        low = lax.ppermute(
            lax.slice_in_dim(block, block.shape[dim] - width, None, axis=dim), axis, forward
        )
        high = lax.ppermute(lax.slice_in_dim(block, 0, width, axis=dim), axis, backward)
        block = jnp.concatenate([low, block, high], axis=dim)
    return block


def wrap_columns(padded, margin):
    return jnp.concatenate([padded[:, :, -margin:], padded, padded[:, :, :margin]], axis=2)


def depthwise(padded, kernel, band_rows, columns):
    kernel_side = math.isqrt(kernel.shape[0])
    summed = jnp.zeros(padded.shape[:1] + (band_rows, columns, padded.shape[3]), jnp.float32)
    for row_off in range(kernel_side):
        for col_off in range(kernel_side):
            window = padded[:, row_off : row_off + band_rows, col_off : col_off + columns, :]
            summed = summed + window.astype(jnp.float32) * kernel[
                kernel_side * row_off + col_off
            ].astype(jnp.float32)
    return summed


def kernel_terms(padded, gradient, kernel_side):
    band_rows, columns = (gradient.shape[1], gradient.shape[2])
    grad_float = gradient.astype(jnp.float32)
    products = []
    for row_off in range(kernel_side):
        for col_off in range(kernel_side):
            window = padded[:, row_off : row_off + band_rows, col_off : col_off + columns, :]
            products.append(jnp.sum(window.astype(jnp.float32) * grad_float, axis=(0, 1, 2)))
    return jnp.stack(products)


def standardize(conv, moments, pixels):
    mean = moments[0] / pixels
    var = moments[1] / pixels - mean * mean
    scale = lax.rsqrt(var + 1e-05)
    return ((conv - mean) * scale, scale)


def per_device(
    x_in, cotangent, land, grid_res, dw_kernel, gain, shift, res_bias, w_in, b_in, w_out, b_out
):
    samples, height, columns, local_chan = x_in.shape
    groups = lax.axis_size("chan")
    width = local_chan * groups
    band_rows = height // groups
    position = lax.axis_index("chan")
    kernel_side = math.isqrt(dw_kernel.shape[0])
    margin = kernel_side // 2
    pixels = float(samples * lax.axis_size("dp") * height * columns)
    chooser = (grid_res[:, None] == jnp.arange(2, dtype=jnp.int32)[None, :]).astype(jnp.float32)
    land_float = land.astype(jnp.float32)[..., None]
    band_land = lax.dynamic_slice_in_dim(land_float, position * band_rows, band_rows, 1)
    x_band, cot_band = (
        lax.all_to_all(x_in, "chan", split_axis=1, concat_axis=3, tiled=True),
        lax.all_to_all(cotangent, "chan", split_axis=1, concat_axis=3, tiled=True),
    )
    padded = wrap_columns(padded_2(x_band, (("chan", 1),), margin), margin)
    conv = depthwise(padded, dw_kernel, band_rows, columns)
    moments = lax.psum(
        (jnp.sum(conv, axis=(0, 1, 2)), jnp.sum(conv * conv, axis=(0, 1, 2))), ("dp", "chan")
    )
    centred, scale = standardize(conv, moments, pixels)
    sample_bias = jnp.sum(chooser[:, :, None] * res_bias[None], axis=1)
    normed = (gain * centred + shift + sample_bias[:, None, None, :]).astype(jnp.bfloat16)
    flat_rows = normed.reshape(-1, width)
    hidden_pre = jnp.dot(flat_rows, w_in, preferred_element_type=jnp.float32) + b_in
    active, active_back = jax.vjp(partial(jax.nn.gelu, approximate=False), hidden_pre)
    active_low = active.astype(jnp.bfloat16)
    branch = jnp.dot(active_low, w_out, preferred_element_type=jnp.float32) + b_out
    result = band_land * (x_band.astype(jnp.float32) + branch.reshape(x_band.shape))
    mixed = lax.all_to_all(
        result.astype(jnp.bfloat16), "chan", split_axis=3, concat_axis=1, tiled=True
    )
    out_grad = (band_land * cot_band.astype(jnp.float32)).astype(jnp.bfloat16).reshape(-1, width)
    g_w_out = lax.dot_general(
        active_low, out_grad, (((0,), (0,)), ((), ())), preferred_element_type=jnp.float32
    )
    g_b_out = jnp.sum(out_grad.astype(jnp.float32), axis=0)
    active_grad = lax.dot_general(
        out_grad, w_out, (((1,), (1,)), ((), ())), preferred_element_type=jnp.float32
    )
    hidden_grad = active_back(active_grad)[0].astype(jnp.bfloat16)
    g_w_in = lax.dot_general(
        flat_rows, hidden_grad, (((0,), (0,)), ((), ())), preferred_element_type=jnp.float32
    )
    g_b_in = jnp.sum(hidden_grad.astype(jnp.float32), axis=0)
    norm_low = lax.dot_general(
        hidden_grad, w_in, (((1,), (1,)), ((), ())), preferred_element_type=jnp.float32
    )
    norm_low = norm_low.astype(jnp.bfloat16).reshape(x_band.shape)
    norm_grad = norm_low.astype(jnp.float32)
    per_sample = jnp.sum(norm_grad, axis=(1, 2))
    part_res = jnp.sum(chooser[:, :, None] * per_sample[:, None, :], axis=0)
    part_shift = jnp.sum(per_sample, axis=0)
    part_gain = jnp.sum(norm_grad * centred, axis=(0, 1, 2))
    total_shift, total_gain = lax.psum((part_shift, part_gain), ("dp", "chan"))
    conv_grad = (gain * scale * (norm_grad - (total_shift + centred * total_gain) / pixels)).astype(
        jnp.bfloat16
    )
    grad_pad = wrap_columns(padded_2(conv_grad, (("chan", 1),), margin), margin)
    transposed = depthwise(grad_pad, dw_kernel[::-1], band_rows, columns)
    g_kernel = kernel_terms(padded, conv_grad, kernel_side)
    band_grad = (band_land * cot_band.astype(jnp.float32) + transposed).astype(jnp.bfloat16)
    x_grad = lax.all_to_all(band_grad, "chan", split_axis=3, concat_axis=1, tiled=True)
    grads = lax.psum(
        (g_kernel, part_gain, part_shift, part_res, g_w_in, g_b_in, g_w_out, g_b_out),
        ("dp", "chan"),
    )
    return (
        mixed,
        x_grad,
        grads[0],
        grads[1],
        grads[2],
        grads[3],
        grads[4],
        grads[5],
        grads[6],
        grads[7],
    )


def solution(mesh):
    placed = (
        P("dp", None, None, "chan"),
        P("dp", None, None, "chan"),
        P("dp", None, None),
        P("dp"),
        P(),
        P(),
        P(),
        P(),
        P(),
        P(),
        P(),
        P(),
    )
    return jax.shard_map(
        per_device,
        mesh=mesh,
        in_specs=placed,
        out_specs=(
            P("dp", None, None, "chan"),
            P("dp", None, None, "chan"),
            P(),
            P(),
            P(),
            P(),
            P(),
            P(),
            P(),
            P(),
        ),
        check_vma=False,
    )
```

profile of v0, /device:TPU:0, one launch (start us, length us, event | category | flops | bytes accessed | tf_op | source)
XLA Modules:
  0.0 1401.3 jit_solution(16229247172743590174)
XLA Ops:
  7.2 4.7 copy.51
  11.9 6.3 all-to-all-start
  18.3 4.7 copy.59
  23.0 81.6 %all-to-all-done = bf16[1,48,360,100]{2,3,0,1:T(8,128)(2,1)} async-done(((bf16[1,48,360,100]{2,3,0,1:T(8,128)(2,1)}), bf16[1,48,360,100]{2,3,0,1:T(8,128)(2,1)}, u32[]{:S(2)}, u32[]{:S(2)}) %all-to-all-start) | async-done | bytes 3456032 | tf_op jit(solution)/shard_map/all_to_all | solution.py:72
  104.6 4.5 all-to-all-start.2
  109.2 4.5 copy.52
  113.6 6.1 all_to_all.49
  119.8 3.7 fusion.185
  123.4 3.5 collective-permute-start
  134.2 61.3 %all-to-all-done.2 = bf16[1,48,360,100]{2,3,0,1:T(8,128)(2,1)} async-done(((bf16[1,48,360,100]{2,3,0,1:T(8,128)(2,1)}), bf16[1,48,360,100]{2,3,0,1:T(8,128)(2,1)}, u32[]{:S(2)}, u32[]{:S(2)}) %all-to-all-start.2) | async-done | bytes 3456032 | tf_op jit(solution)/shard_map/all_to_all | solution.py:73
  195.4 2.6 convert_bitcast_fusion
  198.0 3.0 copy-done.8
  201.1 3.7 copy.60
  204.7 9.0 copy.61
  213.8 3.0 convert_reduce_fusion.1
  217.5 7.8 reshape.833
  225.3 9.9 reshape.834
  235.2 3.2 constant_dynamic-update-slice_fusion.4
  238.4 2.8 constant_dynamic-update-slice_fusion.3
  241.1 2.2 constant_dynamic-update-slice_fusion.5
  243.3 2.5 copy-done.4
  245.8 2.9 fusion.183
  248.9 124.7 %fusion.180 = (f32[800]{0:T(1024)}, f32[800]{0:T(1024)}, f32[1,6,360,800]{2,3,1,0:T(8,128)}) fusion(f32[800]{0:T(1024)} %get-tuple-element.144, bf16[1,12,3,800]{2,3,1,0:T(8,128)(2,1)} %get-tuple-element.163, bf16[1,12,360,800]{2,3,1,0:T(8,128)(2,1)S(1)} %get-tuple-element.174, f32[800]{0:T(1024)} %get-tuple-element.145, f32[800]{0:T(1024)} %get-tuple-element.98, ...), kind=kLoop, calls=%fused_computation.425 | loop fusion | flops 475198400 | bytes 38294400 | tf_op jit(solution)/shard_map/reduce_sum | solution.py:78
  373.6 38.6 %all-reduce.1 = (f32[800]{0:T(1024)S(1)}, f32[800]{0:T(1024)S(1)}) all-reduce(f32[800]{0:T(1024)} %get-tuple-element.92, f32[800]{0:T(1024)} %get-tuple-element.91), channel_id=1, replica_groups=mesh['dp'=4,'chan'=8] {'dp','chan'}, use_global_device_ids=true, to_apply=%region_3.0 | all-reduce | flops 1600 | bytes 12800 | tf_op jit(solution)/shard_map/psum | solution.py:77
  414.1 5.4 add_convert_fusion.2
  419.5 6.2 copy.53
  425.7 77.8 %multiply_convert_fusion = (bf16[2160,3200]{1,0:T(8,128)(2,1)}, f32[2160,3200]{1,0:T(8,128)}, f32[2160,3200]{1,0:T(8,128)}) fusion(f32[3200]{0:T(1024)S(1)} %copy-done.81, bf16[2160,800]{1,0:T(8,128)(2,1)} %bitcast.54, bf16[800,3200]{1,0:T(8,128)(2,1)} %param.20), kind=kOutput, calls=%fused_computation.95 | convolution fusion | flops 11515392000 | bytes 77708800 | tf_op jit(solution)/shard_map/dot_general | solution.py:84
  503.5 30.0 %convert_reduce_fusion = (f32[3200]{0:T(1024)S(1)}, bf16[2160,3200]{1,0:T(8,128)(2,1)}) fusion(f32[2160,3200]{1,0:T(8,128)} %get-tuple-element.158, f32[2160,3200]{1,0:T(8,128)} %get-tuple-element.178, bf16[3200,800]{0,1:T(8,128)(2,1)} %param.22, f32[2160,800]{1,0:T(8,128)} %reshape.834, f32[2160]{0:T(1024)S(1)} %copy-done.75), kind=kOutput, calls=%fused_computation.93 | convolution fusion | flops 11173244928 | bytes 81173440 | tf_op jit(solution)/shard_map/dot_general | solution.py:97
  533.5 18.7 %fusion.186 = (f32[800]{0:T(1024)S(1)}, f32[2160,800]{0,1:T(8,128)}) fusion(bf16[2160,3200]{1,0:T(8,128)(2,1)} %get-tuple-element.182, bf16[800,3200]{1,0:T(8,128)(2,1)} %param.20), kind=kOutput, calls=%fused_computation.429 | convolution fusion | flops 11064384512 | bytes 25859200 | tf_op jit(solution)/shard_map/dot_general | solution.py:105
  552.3 8.4 copy.62
  560.7 8.5 copy.64
  569.2 6.6 multiply_reduce_fusion
  575.8 42.8 %all-reduce = (f32[800]{0:T(1024)S(1)}, f32[800]{0:T(1024)S(1)}, f32[2,800]{1,0:T(2,128)}, f32[3200]{0:T(1024)}, f32[800]{0:T(1024)}) all-reduce(f32[800]{0:T(1024)S(1)} %multiply_reduce_fusion, f32[800]{0:T(1024)S(1)} %get-tuple-element.179, f32[2,800]{1,0:T(2,128)S(1)} %broadcast_multiply_fusion, ...), channel_id=1, replica_groups=mesh['dp'=4,'chan'=8] {'dp','chan'}, use_global_device_ids=true, to_apply=%region_8.0 | all-reduce | flops 7200 | bytes 57600 | tf_op jit(solution)/shard_map/psum | solution.py:114
  618.6 30.0 %fusion.128 = (f32[800]{0:T(1024)S(1)}, f32[800]{0:T(1024)S(1)}, f32[800]{0:T(1024)S(1)}, f32[800]{0:T(1024)S(1)}, f32[800]{0:T(1024)S(1)}, /*index=5*/f32[800]{0:T(1024)S(1)}, bf16[1,6,360,800]{2,3,1,0:T(8,128)(2,1)S(1)}) fusion(bf16[1,12,3,800]{2,3,1,0:T(8,128)(2,1)} %get-tuple-element.163, bf16[1,12,360,800]{2,3,1,0:T(8,128)(2,1)} %copy-done, ...), kind=kLoop, calls=%fused_computation.285 | loop fusion | flops 77755200 | bytes 24284800 | tf_op jit(solution)/shard_map/reduce_sum | solution.py:46
  648.7 6.7 fusion.127
  655.5 20.8 %fusion.130 = (f32[800]{0:T(1024)S(1)}, f32[800]{0:T(1024)S(1)}, f32[800]{0:T(1024)S(1)}, f32[800]{0:T(1024)S(1)}, f32[800]{0:T(1024)S(1)}, /*index=5*/f32[800]{0:T(1024)S(1)}, f32[800]{0:T(1024)S(1)}) fusion(bf16[1,6,360,800]{2,3,1,0:T(8,128)(2,1)S(1)} %get-tuple-element.156, bf16[1,12,3,800]{2,3,1,0:T(8,128)(2,1)S(1)} %copy-done.7, ...), kind=kLoop, calls=%fused_computation.287 | loop fusion | flops 69114400 | bytes 13904000 | tf_op jit(solution)/shard_map/reduce_sum | solution.py:46
  676.3 19.8 %fusion.129 = (f32[800]{0:T(1024)S(1)}, f32[800]{0:T(1024)S(1)}, f32[800]{0:T(1024)S(1)}, f32[800]{0:T(1024)S(1)}, f32[800]{0:T(1024)S(1)}, /*index=5*/f32[800]{0:T(1024)S(1)}) fusion(bf16[1,6,360,800]{2,3,1,0:T(8,128)(2,1)S(1)} %get-tuple-element.156, bf16[1,12,3,800]{2,3,1,0:T(8,128)(2,1)S(1)} %copy-done.7, bf16[1,12,360,800]{2,3,1,0:T(8,128)(2,1)S(1)} %bitcast.41), kind=kLoop, calls=%fused_computation.286 | loop fusion | flops 63931200 | bytes 10444800 | tf_op jit(solution)/shard_map/reduce_sum | solution.py:46
  696.2 18.4 %fusion.123 = (f32[800]{0:T(1024)S(1)}, f32[800]{0:T(1024)S(1)}, f32[800]{0:T(1024)S(1)}, f32[800]{0:T(1024)S(1)}, f32[800]{0:T(1024)S(1)}, /*index=5*/f32[800]{0:T(1024)S(1)}) fusion(bf16[1,6,360,800]{2,3,1,0:T(8,128)(2,1)S(1)} %get-tuple-element.156, bf16[1,12,3,800]{2,3,1,0:T(8,128)(2,1)S(1)} %copy-done.7, bf16[1,12,360,800]{2,3,1,0:T(8,128)(2,1)S(1)} %bitcast.41, ...), kind=kLoop, calls=%fused_computation.280 | loop fusion | flops 63931200 | bytes 10502400 | tf_op jit(solution)/shard_map/reduce_sum | solution.py:46
  714.6 16.9 %fusion.124 = (f32[800]{0:T(1024)S(1)}, f32[800]{0:T(1024)S(1)}, f32[800]{0:T(1024)S(1)}, f32[800]{0:T(1024)S(1)}, f32[800]{0:T(1024)S(1)}, /*index=5*/f32[800]{0:T(1024)S(1)}) fusion(bf16[1,6,360,800]{2,3,1,0:T(8,128)(2,1)S(1)} %get-tuple-element.156, bf16[1,12,3,800]{2,3,1,0:T(8,128)(2,1)S(1)} %copy-done.6, bf16[1,12,360,800]{2,3,1,0:T(8,128)(2,1)S(1)} %bitcast.41), kind=kLoop, calls=%fused_computation.281 | loop fusion | flops 63931200 | bytes 10444800 | tf_op jit(solution)/shard_map/reduce_sum | solution.py:46
  731.5 17.5 %fusion.126 = (f32[800]{0:T(1024)S(1)}, f32[800]{0:T(1024)S(1)}, f32[800]{0:T(1024)S(1)}, f32[800]{0:T(1024)S(1)}, f32[800]{0:T(1024)S(1)}, /*index=5*/f32[800]{0:T(1024)S(1)}) fusion(bf16[1,6,360,800]{2,3,1,0:T(8,128)(2,1)S(1)} %get-tuple-element.156, bf16[1,12,360,800]{2,3,1,0:T(8,128)(2,1)S(1)} %bitcast.41, bf16[1,12,3,800]{2,3,1,0:T(8,128)(2,1)S(1)} %copy-done.6), kind=kLoop, calls=%fused_computation.283 | loop fusion | flops 63931200 | bytes 10444800 | tf_op jit(solution)/shard_map/reduce_sum | solution.py:46
  749.0 17.4 %fusion.125 = (f32[800]{0:T(1024)S(1)}, f32[800]{0:T(1024)S(1)}, f32[800]{0:T(1024)S(1)}, f32[800]{0:T(1024)S(1)}, f32[800]{0:T(1024)S(1)}, /*index=5*/f32[800]{0:T(1024)S(1)}) fusion(bf16[1,6,360,800]{2,3,1,0:T(8,128)(2,1)S(1)} %get-tuple-element.156, bf16[1,12,3,800]{2,3,1,0:T(8,128)(2,1)S(1)} %copy-done.6, bf16[1,12,360,800]{2,3,1,0:T(8,128)(2,1)S(1)} %bitcast.41), kind=kLoop, calls=%fused_computation.282 | loop fusion | flops 63931200 | bytes 10444800 | tf_op jit(solution)/shard_map/reduce_sum | solution.py:46
  766.4 2.3 fusion.184
  768.7 22.1 %fusion.179 = f32[3200,800]{0,1:T(8,128)} fusion(bf16[2160,3200]{1,0:T(8,128)(2,1)} %get-tuple-element.157, f32[2160,800]{1,0:T(8,128)} %reshape.834, f32[2160]{0:T(1024)S(1)} %copy-done.75), kind=kOutput, calls=%fused_computation.424 | convolution fusion | flops 11062656000 | bytes 30984640 | tf_op jit(solution)/shard_map/dot_general | solution.py:93
  790.8 16.8 %convolution_add_fusion.1 = f32[2160,800]{0,1:T(8,128)} fusion(bf16[2160,3200]{1,0:T(8,128)(2,1)} %get-tuple-element.157, bf16[3200,800]{0,1:T(8,128)(2,1)S(1)} %bitcast.57, f32[800]{0:T(1024)S(1)} %copy-done.82), kind=kOutput, calls=%fused_computation.304 | convolution fusion | flops 11060928512 | bytes 25859200 | tf_op jit(solution)/shard_map/dot_general | solution.py:87
  807.5 8.4 copy.54
  815.9 8.5 copy.55
  824.4 5.1 fusion.56
  829.5 3.5 copy.56
  833.1 4.6 all-to-all-start.1
  838.4 2.3 collective-permute-start.2
  842.0 4.5 stack.199
  846.6 20.4 %fusion.187 = f32[800,3200]{1,0:T(8,128)} fusion(bf16[2160,800]{1,0:T(8,128)(2,1)} %bitcast.55, bf16[2160,3200]{1,0:T(8,128)(2,1)} %get-tuple-element.182), kind=kOutput, calls=%fused_computation.430 | convolution fusion | flops 11059200000 | bytes 27520000 | tf_op jit(solution)/shard_map/dot_general | solution.py:101
  867.4 15.4 %fusion.132 = (bf16[1,12,363,800]{2,3,1,0:T(8,128)(2,1)S(1)}, bf16[1,12,363,800]{2,3,1,0:T(8,128)(2,1)}) fusion(bf16[1,3,360,800]{2,3,1,0:T(8,128)(2,1)} %collective-permute-done.3, bf16[1,6,360,800]{2,3,1,0:T(8,128)(2,1)} %copy-done.1, bf16[1,3,360,800]{2,3,1,0:T(8,128)(2,1)S(1)} %collective-permute-done.2), kind=kLoop, calls=%fused_computation.292 | loop fusion | flops 83635200 | bytes 20851200 | tf_op jit(solution)/shard_map/concatenate | solution.py:24
  883.2 93.0 %add_convert_fusion.1 = bf16[1,6,360,800]{2,3,1,0:T(8,128)(2,1)} fusion(f32[1,6,360,800]{2,3,1,0:T(8,128)} %reshape.833, bf16[1,6,360,800]{2,3,1,0:T(8,128)(2,1)} %copy-done.1, bf16[1,3,360,800]{2,3,1,0:T(8,128)(2,1)} %collective-permute-done.3, bf16[1,3,360,800]{2,3,1,0:T(8,128)(2,1)S(1)} %collective-permute-done.2, ...), kind=kLoop, calls=%fused_computation.294 | loop fusion | flops 267840000 | bytes 162597440 | tf_op jit(solution)/shard_map/convert_element_type | solution.py:121
  976.2 5.6 copy.65
  981.8 180.0 %all-to-all-start.3 = ((bf16[1,6,360,800]{2,1,0,3:T(8,128)(2,1)}), bf16[1,6,360,800]{2,1,0,3:T(8,128)(2,1)}, u32[]{:S(2)}, u32[]{:S(2)}) async-start(bf16[1,6,360,800]{2,1,0,3:T(8,128)(2,1)} %copy.65), calls=%async_computation.3 | async-start | bytes 9830400 | tf_op jit(solution)/shard_map/all_to_all | solution.py:122
  1161.8 3.0 copy.75
  1165.2 2.3 copy.68
  1167.5 150.5 %all-to-all-done.3 = bf16[1,6,360,800]{2,1,0,3:T(8,128)(2,1)} async-done(((bf16[1,6,360,800]{2,1,0,3:T(8,128)(2,1)}), bf16[1,6,360,800]{2,1,0,3:T(8,128)(2,1)}, u32[]{:S(2)}, u32[]{:S(2)}) %all-to-all-start.3) | async-done | bytes 3456032 | tf_op jit(solution)/shard_map/all_to_all | solution.py:122
  1318.0 3.0 copy.74
  1321.4 2.3 copy.69
  1323.7 55.8 %all-reduce.5.cloned.1.call-done = (f32[49,800]{1,0:T(8,128)}, f32[800,3200]{1,0:T(8,128)}, f32[3200,800]{0,1:T(8,128)}) async-done(((f32[49,800]{1,0:T(8,128)}, f32[800,3200]{1,0:T(8,128)}, f32[3200,800]{0,1:T(8,128)}), (f32[49,800]{1,0:T(8,128)}, f32[800,3200]{1,0:T(8,128)}, f32[3200,800]{0,1:T(8,128)})) %all-reduce.5.cloned.1.call-update) | async-done | bytes 20636816 | tf_op jit(solution)/shard_map/psum | solution.py:123
  1381.2 8.7 copy.85
  1390.0 4.0 copy.86
  (263 shorter events, 13.5 us)
Async XLA Ops:
  11.9 92.7 %all-to-all-start = ((bf16[1,48,360,100]{2,3,0,1:T(8,128)(2,1)}), bf16[1,48,360,100]{2,3,0,1:T(8,128)(2,1)}, u32[]{:S(2)}, u32[]{:S(2)}) async-start(bf16[1,48,360,100]{2,3,0,1:T(8,128)(2,1)} %copy.51), calls=%async_computation | async-start | bytes 7667712 | tf_op jit(solution)/shard_map/all_to_all | solution.py:72
  104.6 90.8 %all-to-all-start.2 = ((bf16[1,48,360,100]{2,3,0,1:T(8,128)(2,1)}), bf16[1,48,360,100]{2,3,0,1:T(8,128)(2,1)}, u32[]{:S(2)}, u32[]{:S(2)}) async-start(bf16[1,48,360,100]{2,3,0,1:T(8,128)(2,1)} %copy.59), calls=%async_computation.2 | async-start | bytes 7667712 | tf_op jit(solution)/shard_map/all_to_all | solution.py:73
  123.4 111.7 %collective-permute-start = (bf16[1,3,360,800]{2,3,1,0:T(8,128)(2,1)}, bf16[1,3,360,800]{2,3,1,0:T(8,128)(2,1)}, u32[]{:S(2)}, u32[]{:S(2)}) collective-permute-start(bf16[1,3,360,800]{2,3,1,0:T(8,128)(2,1)} %get-tuple-element.170), channel_id=1, source_target_pairs={{0,1},{1,2},{2,3},{3,4},{4,5},{5,6},{6,7},{8,9},{9,10},{10,11},{11... | collective-permute-start | bytes 5184008 | tf_op jit(solution)/shard_map/ppermute | solution.py:15
  128.4 85.4 %copy-start.10 = (f32[6,360]{1,0:T(8,128)}, f32[6,360]{1,0:T(8,128)S(1)}, u32[]{:S(2)}) copy-start(f32[6,360]{1,0:T(8,128)S(1)} %fusion.198) | copy-start | bytes 25924
  129.8 111.4 %collective-permute-start.1 = (bf16[1,3,360,800]{2,3,1,0:T(8,128)(2,1)S(1)}, bf16[1,3,360,800]{2,3,1,0:T(8,128)(2,1)}, u32[]{:S(2)}, u32[]{:S(2)}) collective-permute-start(bf16[1,3,360,800]{2,3,1,0:T(8,128)(2,1)S(1)} %get-tuple-element.169), channel_id=1, source_target_pairs={{1,0},{2,1},{3,2},{4,3},{5,4},{6,5},{7,6},{9,8},{10,9},{11,10},{12... | collective-permute-start | bytes 5184008 | tf_op jit(solution)/shard_map/ppermute | solution.py:18
  133.3 115.5 %copy-start.16 = (f32[800]{0:T(1024)}, f32[800]{0:T(1024)S(1)}, u32[]{:S(2)}) copy-start(f32[800]{0:T(1024)S(1)} %get-tuple-element.116) | copy-start | bytes 9604
  133.3 115.5 %copy-start.18 = (f32[800]{0:T(1024)}, f32[800]{0:T(1024)S(1)}, u32[]{:S(2)}) copy-start(f32[800]{0:T(1024)S(1)} %get-tuple-element.117) | copy-start | bytes 9604
  133.3 115.5 %copy-start.20 = (f32[800]{0:T(1024)}, f32[800]{0:T(1024)S(1)}, u32[]{:S(2)}) copy-start(f32[800]{0:T(1024)S(1)} %get-tuple-element.118) | copy-start | bytes 9604
  133.3 115.5 %copy-start.22 = (f32[800]{0:T(1024)}, f32[800]{0:T(1024)S(1)}, u32[]{:S(2)}) copy-start(f32[800]{0:T(1024)S(1)} %get-tuple-element.119) | copy-start | bytes 9604
  133.3 115.5 %copy-start.24 = (f32[800]{0:T(1024)}, f32[800]{0:T(1024)S(1)}, u32[]{:S(2)}) copy-start(f32[800]{0:T(1024)S(1)} %get-tuple-element.120) | copy-start | bytes 9604
  133.3 115.5 %copy-start.26 = (f32[800]{0:T(1024)}, f32[800]{0:T(1024)S(1)}, u32[]{:S(2)}) copy-start(f32[800]{0:T(1024)S(1)} %get-tuple-element.121) | copy-start | bytes 9604
  133.3 115.5 %copy-start.28 = (f32[800]{0:T(1024)}, f32[800]{0:T(1024)S(1)}, u32[]{:S(2)}) copy-start(f32[800]{0:T(1024)S(1)} %get-tuple-element.122) | copy-start | bytes 9604
  133.3 115.5 %copy-start.30 = (f32[800]{0:T(1024)}, f32[800]{0:T(1024)S(1)}, u32[]{:S(2)}) copy-start(f32[800]{0:T(1024)S(1)} %get-tuple-element.123) | copy-start | bytes 9604
  133.3 115.5 %copy-start.32 = (f32[800]{0:T(1024)}, f32[800]{0:T(1024)S(1)}, u32[]{:S(2)}) copy-start(f32[800]{0:T(1024)S(1)} %get-tuple-element.124) | copy-start | bytes 9604
  133.3 115.5 %copy-start.34 = (f32[800]{0:T(1024)}, f32[800]{0:T(1024)S(1)}, u32[]{:S(2)}) copy-start(f32[800]{0:T(1024)S(1)} %get-tuple-element.125) | copy-start | bytes 9604
  133.3 115.5 %copy-start.36 = (f32[800]{0:T(1024)}, f32[800]{0:T(1024)S(1)}, u32[]{:S(2)}) copy-start(f32[800]{0:T(1024)S(1)} %get-tuple-element.126) | copy-start | bytes 9604
  133.3 115.5 %copy-start.38 = (f32[800]{0:T(1024)}, f32[800]{0:T(1024)S(1)}, u32[]{:S(2)}) copy-start(f32[800]{0:T(1024)S(1)} %get-tuple-element.127) | copy-start | bytes 9604
  133.3 115.5 %copy-start.40 = (f32[800]{0:T(1024)}, f32[800]{0:T(1024)S(1)}, u32[]{:S(2)}) copy-start(f32[800]{0:T(1024)S(1)} %get-tuple-element.128) | copy-start | bytes 9604
  133.4 115.5 %copy-start.42 = (f32[800]{0:T(1024)}, f32[800]{0:T(1024)S(1)}, u32[]{:S(2)}) copy-start(f32[800]{0:T(1024)S(1)} %get-tuple-element.129) | copy-start | bytes 9604
  133.4 115.5 %copy-start.44 = (f32[800]{0:T(1024)}, f32[800]{0:T(1024)S(1)}, u32[]{:S(2)}) copy-start(f32[800]{0:T(1024)S(1)} %get-tuple-element.130) | copy-start | bytes 9604
  133.4 115.5 %copy-start.46 = (f32[800]{0:T(1024)}, f32[800]{0:T(1024)S(1)}, u32[]{:S(2)}) copy-start(f32[800]{0:T(1024)S(1)} %get-tuple-element.131) | copy-start | bytes 9604
  133.4 115.5 %copy-start.48 = (f32[800]{0:T(1024)}, f32[800]{0:T(1024)S(1)}, u32[]{:S(2)}) copy-start(f32[800]{0:T(1024)S(1)} %get-tuple-element.132) | copy-start | bytes 9604
  245.8 127.9 %copy-start = (bf16[1,12,360,800]{2,3,1,0:T(8,128)(2,1)}, bf16[1,12,360,800]{2,3,1,0:T(8,128)(2,1)S(1)}, u32[]{:S(2)}) copy-start(bf16[1,12,360,800]{2,3,1,0:T(8,128)(2,1)S(1)} %get-tuple-element.174) | copy-start | bytes 20736004
  248.7 124.9 %copy-start.5 = (bf16[1,12,3,800]{2,3,1,0:T(8,128)(2,1)}, bf16[1,12,3,800]{2,3,1,0:T(8,128)(2,1)S(1)}, u32[]{:S(2)}) copy-start(bf16[1,12,3,800]{2,3,1,0:T(8,128)(2,1)S(1)} %get-tuple-element.162) | copy-start | bytes 172804
  425.7 77.8 %copy-start.75 = (f32[2160]{0:T(1024)S(1)}, f32[2160]{0:T(1024)}, u32[]{:S(2)}) copy-start(f32[2160]{0:T(1024)} %mul.1107) | copy-start | bytes 25924
  533.5 18.7 %copy-start.80 = (f32[2]{0:T(128)S(1)}, f32[2]{0:T(128)}, u32[]{:S(2)}) copy-start(f32[2]{0:T(128)} %copy-done.79) | copy-start | bytes 28
  569.2 49.4 %copy-start.73 = (f32[800]{0:T(1024)S(1)}, f32[800]{0:T(1024)}, u32[]{:S(2)}) copy-start(f32[800]{0:T(1024)} %get-tuple-element.175) | copy-start | bytes 9604
  569.2 86.3 %slice-start = ((s8[7372800]{0:T(1024)(128)(4,1)}), s8[3178496]{0:T(1024)(128)(4,1)S(1)}, s32[]{:S(2)}) async-start(s8[7372800]{0:T(1024)(128)(4,1)} %bitcast.40), calls=%async_computation.5 | async-start | bytes 6356992
  618.6 30.0 %copy-start.77 = (f32[800]{0:T(1024)}, f32[800]{0:T(1024)S(1)}, u32[]{:S(2)}) copy-start(f32[800]{0:T(1024)S(1)} %get-tuple-element.186) | copy-start | bytes 9604
  618.6 30.0 %copy-start.78 = (f32[800]{0:T(1024)}, f32[800]{0:T(1024)S(1)}, u32[]{:S(2)}) copy-start(f32[800]{0:T(1024)S(1)} %get-tuple-element.187) | copy-start | bytes 9604
  618.6 30.1 %slice-start.2 = ((s8[5529600]{0:T(1024)(128)(4,1)}), s8[4194304]{0:T(1024)(128)(4,1)S(1)}, s32[]{:S(2)}) async-start(s8[5529600]{0:T(1024)(128)(4,1)} %bitcast.42), calls=%async_computation.7 | async-start | bytes 8388608
  618.6 30.1 %slice-start.4 = ((s8[5529600]{0:T(1024)(128)(4,1)}), s8[4194304]{0:T(1024)(128)(4,1)S(1)}, s32[]{:S(2)}) async-start(s8[5529600]{0:T(1024)(128)(4,1)} %bitcast.44), calls=%async_computation.9 | async-start | bytes 8388608
  618.6 30.1 %slice-start.3 = ((s8[5529600]{0:T(1024)(128)(4,1)}), s8[1335296]{0:T(1024)(128)(4,1)S(1)}, s32[]{:S(2)}) async-start(s8[5529600]{0:T(1024)(128)(4,1)} %bitcast.42), calls=%async_computation.8 | async-start | bytes 2670592
  618.6 30.1 %slice-start.5 = ((s8[5529600]{0:T(1024)(128)(4,1)}), s8[1335296]{0:T(1024)(128)(4,1)S(1)}, s32[]{:S(2)}) async-start(s8[5529600]{0:T(1024)(128)(4,1)} %bitcast.44), calls=%async_computation.10 | async-start | bytes 2670592
  618.6 36.8 %slice-start.1 = ((s8[7372800]{0:T(1024)(128)(4,1)}), s8[4194304]{0:T(1024)(128)(4,1)S(1)}, s32[]{:S(2)}) async-start(s8[7372800]{0:T(1024)(128)(4,1)} %bitcast.40), calls=%async_computation.6 | async-start | bytes 8388608
  648.6 117.8 %copy-start.1 = (bf16[1,6,360,800]{2,3,1,0:T(8,128)(2,1)}, bf16[1,6,360,800]{2,3,1,0:T(8,128)(2,1)S(1)}, u32[]{:S(2)}) copy-start(bf16[1,6,360,800]{2,3,1,0:T(8,128)(2,1)S(1)} %get-tuple-element.156) | copy-start | bytes 10368004
  676.3 19.8 %copy-start.6 = (bf16[1,12,3,800]{2,3,1,0:T(8,128)(2,1)S(1)}, bf16[1,12,3,800]{2,3,1,0:T(8,128)(2,1)}, u32[]{:S(2)}) copy-start(bf16[1,12,3,800]{2,3,1,0:T(8,128)(2,1)} %copy-done.5) | copy-start | bytes 172804
  766.4 24.3 %slice-start.9 = ((s8[5120000]{0:T(1024)(128)(4,1)}), s8[4194304]{0:T(1024)(128)(4,1)S(1)}, s32[]{:S(2)}) async-start(s8[5120000]{0:T(1024)(128)(4,1)} %bitcast.56), calls=%async_computation.14 | async-start | bytes 8388608
  768.7 22.1 %slice-start.10 = ((s8[5120000]{0:T(1024)(128)(4,1)}), s8[925696]{0:T(1024)(128)(4,1)S(1)}, s32[]{:S(2)}) async-start(s8[5120000]{0:T(1024)(128)(4,1)} %bitcast.56), calls=%async_computation.15 | async-start | bytes 1851392
  768.7 22.1 %copy-start.82 = (f32[800]{0:T(1024)S(1)}, f32[800]{0:T(1024)}, u32[]{:S(2)}) copy-start(f32[800]{0:T(1024)} %param.23) | copy-start | bytes 9604
  833.1 148.7 %all-to-all-start.1 = ((bf16[1,6,360,800]{2,1,0,3:T(8,128)(2,1)}), bf16[1,6,360,800]{2,1,0,3:T(8,128)(2,1)}, u32[]{:S(2)}, u32[]{:S(2)}) async-start(bf16[1,6,360,800]{2,1,0,3:T(8,128)(2,1)} %copy.56), calls=%async_computation.1 | async-start | bytes 9830400 | tf_op jit(solution)/shard_map/all_to_all | solution.py:89
  837.7 541.7 %all-reduce.5.cloned.1.call-start = ((), (), s32[]{:S(2)}) async-start(), calls=%async_computation.4 | async-start | bytes 41361408 | tf_op jit(solution)/shard_map/psum | solution.py:123
  838.4 29.0 %collective-permute-start.2 = (bf16[1,3,360,800]{2,3,1,0:T(8,128)(2,1)}, bf16[1,3,360,800]{2,3,1,0:T(8,128)(2,1)S(1)}, u32[]{:S(2)}, u32[]{:S(2)}) collective-permute-start(bf16[1,3,360,800]{2,3,1,0:T(8,128)(2,1)} %get-tuple-element.164), channel_id=1, source_target_pairs={{0,1},{1,2},{2,3},{3,4},{4,5},{5,6},{6,7},{8,9},{9,10},{10,11},{11... | collective-permute-start | bytes 5184008 | tf_op jit(solution)/shard_map/ppermute | solution.py:15
  840.7 26.7 %collective-permute-start.3 = (bf16[1,3,360,800]{2,3,1,0:T(8,128)(2,1)}, bf16[1,3,360,800]{2,3,1,0:T(8,128)(2,1)}, u32[]{:S(2)}, u32[]{:S(2)}) collective-permute-start(bf16[1,3,360,800]{2,3,1,0:T(8,128)(2,1)} %get-tuple-element.165), channel_id=1, source_target_pairs={{1,0},{2,1},{3,2},{4,3},{5,4},{6,5},{7,6},{9,8},{10,9},{11,10},{12... | collective-permute-start | bytes 5184008 | tf_op jit(solution)/shard_map/ppermute | solution.py:18
  867.0 15.8 %copy-start.17 = (f32[800]{0:T(1024)S(1)}, f32[800]{0:T(1024)}, u32[]{:S(2)}) copy-start(f32[800]{0:T(1024)} %copy-done.16) | copy-start | bytes 9604
  867.0 15.8 %copy-start.19 = (f32[800]{0:T(1024)S(1)}, f32[800]{0:T(1024)}, u32[]{:S(2)}) copy-start(f32[800]{0:T(1024)} %copy-done.18) | copy-start | bytes 9604
  867.0 15.8 %copy-start.21 = (f32[800]{0:T(1024)S(1)}, f32[800]{0:T(1024)}, u32[]{:S(2)}) copy-start(f32[800]{0:T(1024)} %copy-done.20) | copy-start | bytes 9604
  867.0 15.8 %copy-start.23 = (f32[800]{0:T(1024)S(1)}, f32[800]{0:T(1024)}, u32[]{:S(2)}) copy-start(f32[800]{0:T(1024)} %copy-done.22) | copy-start | bytes 9604
  867.0 15.8 %copy-start.25 = (f32[800]{0:T(1024)S(1)}, f32[800]{0:T(1024)}, u32[]{:S(2)}) copy-start(f32[800]{0:T(1024)} %copy-done.24) | copy-start | bytes 9604
  867.0 15.8 %copy-start.27 = (f32[800]{0:T(1024)S(1)}, f32[800]{0:T(1024)}, u32[]{:S(2)}) copy-start(f32[800]{0:T(1024)} %copy-done.26) | copy-start | bytes 9604
  867.0 15.8 %copy-start.29 = (f32[800]{0:T(1024)S(1)}, f32[800]{0:T(1024)}, u32[]{:S(2)}) copy-start(f32[800]{0:T(1024)} %copy-done.28) | copy-start | bytes 9604
  867.0 15.8 %copy-start.31 = (f32[800]{0:T(1024)S(1)}, f32[800]{0:T(1024)}, u32[]{:S(2)}) copy-start(f32[800]{0:T(1024)} %copy-done.30) | copy-start | bytes 9604
  867.0 15.8 %copy-start.33 = (f32[800]{0:T(1024)S(1)}, f32[800]{0:T(1024)}, u32[]{:S(2)}) copy-start(f32[800]{0:T(1024)} %copy-done.32) | copy-start | bytes 9604
  867.0 15.8 %copy-start.35 = (f32[800]{0:T(1024)S(1)}, f32[800]{0:T(1024)}, u32[]{:S(2)}) copy-start(f32[800]{0:T(1024)} %copy-done.34) | copy-start | bytes 9604
  867.1 15.8 %copy-start.37 = (f32[800]{0:T(1024)S(1)}, f32[800]{0:T(1024)}, u32[]{:S(2)}) copy-start(f32[800]{0:T(1024)} %copy-done.36) | copy-start | bytes 9604
  867.1 15.8 %copy-start.39 = (f32[800]{0:T(1024)S(1)}, f32[800]{0:T(1024)}, u32[]{:S(2)}) copy-start(f32[800]{0:T(1024)} %copy-done.38) | copy-start | bytes 9604
  867.1 15.8 %copy-start.41 = (f32[800]{0:T(1024)S(1)}, f32[800]{0:T(1024)}, u32[]{:S(2)}) copy-start(f32[800]{0:T(1024)} %copy-done.40) | copy-start | bytes 9604
  867.1 15.8 %copy-start.43 = (f32[800]{0:T(1024)S(1)}, f32[800]{0:T(1024)}, u32[]{:S(2)}) copy-start(f32[800]{0:T(1024)} %copy-done.42) | copy-start | bytes 9604
  867.1 15.8 %copy-start.45 = (f32[800]{0:T(1024)S(1)}, f32[800]{0:T(1024)}, u32[]{:S(2)}) copy-start(f32[800]{0:T(1024)} %copy-done.44) | copy-start | bytes 9604
  867.1 15.8 %copy-start.47 = (f32[800]{0:T(1024)S(1)}, f32[800]{0:T(1024)}, u32[]{:S(2)}) copy-start(f32[800]{0:T(1024)} %copy-done.46) | copy-start | bytes 9604
  867.1 15.8 %copy-start.49 = (f32[800]{0:T(1024)S(1)}, f32[800]{0:T(1024)}, u32[]{:S(2)}) copy-start(f32[800]{0:T(1024)} %copy-done.48) | copy-start | bytes 9604
  867.1 15.8 %copy-start.50 = (f32[800]{0:T(1024)S(1)}, f32[800]{0:T(1024)}, u32[]{:S(2)}) copy-start(f32[800]{0:T(1024)} %get-tuple-element.133) | copy-start | bytes 9604
  867.1 15.8 %copy-start.51 = (f32[800]{0:T(1024)S(1)}, f32[800]{0:T(1024)}, u32[]{:S(2)}) copy-start(f32[800]{0:T(1024)} %get-tuple-element.134) | copy-start | bytes 9604
  981.8 336.1 %all-to-all-start.3 = ((bf16[1,6,360,800]{2,1,0,3:T(8,128)(2,1)}), bf16[1,6,360,800]{2,1,0,3:T(8,128)(2,1)}, u32[]{:S(2)}, u32[]{:S(2)}) async-start(bf16[1,6,360,800]{2,1,0,3:T(8,128)(2,1)} %copy.65), calls=%async_computation.3 | async-start | bytes 9830400 | tf_op jit(solution)/shard_map/all_to_all | solution.py:122
  (39 other events, 459.6 us)
Sparse Core Ops, SparseCore 0:
  867.1 512.3 all-reduce.4
where the time goes:
time: 1410 us; the launch traced here: 1400 us
  other arithmetic  409 us (29%)
  waiting for transfers between devices  349 us (25%)
  starting transfers between devices  204 us (14%)
  matrix products  186 us (13%)
  local copies, waits for them, and re-layouts  155 us (11%)
  blocking collectives  81.3 us (6%)
  between operations  16.8 us (1%)
    all_to_all x1, starting transfers between devices, per_device(): lax.all_to_all(band_grad, 'chan', split_axis=3, concat_axis=1, tiled=True)  180 us
    all_to_all x1, waiting for transfers between devices, per_device(): lax.all_to_all(band_grad, 'chan', split_axis=3, concat_axis=1, tiled=True)  150 us
    reduce_sum x8, other arithmetic, kernel_terms(): jnp.sum(window.astype(jnp.float32) * grad_float, axis=(0, 1, 2))  148 us
    reduce_sum x1, other arithmetic, per_device(): jnp.sum(conv, axis=(0, 1, 2))  125 us
    convert_element_type x1, other arithmetic, per_device(): (band_land * cot_band.astype(jnp.float32) + transposed).astype(jnp.bfloat16)  93 us
    all_to_all x1, waiting for transfers between devices, per_device(): lax.all_to_all(x_in, 'chan', split_axis=1, concat_axis=3, tiled=True)  81.6 us
    dot_general x1, matrix products, per_device(): jnp.dot(flat_rows, w_in, preferred_element_type=jnp.float32) + b_in  77.8 us
    all_to_all x1, waiting for transfers between devices, per_device(): lax.all_to_all(cotangent, 'chan', split_axis=1, concat_axis=3, tiled=True)  61.3 us
  transfers between devices with their start and end apart: 9, of which 4 were waited for; matrix products, arithmetic and copies ran while one was open for 15% of the time, Pallas kernels for 0%

commit v1 on v0

v1 whole, which is shorter than its diff:
```python
from functools import partial
import math

import jax
import jax.numpy as jnp
from jax import lax
from jax.experimental import pallas as pl
from jax.experimental.pallas import tpu as pltpu
from jax.sharding import PartitionSpec as P

LANES = 128
SUBL = 8
VMEM_LIMIT = 56 * 1024 * 1024
CHAN = ("pair", "core")
CORES = 2
F32 = jnp.float32
BF16 = jnp.bfloat16


def round_up(value, step):
    return (value + step - 1) // step * step


def block_of(total, most):
    return max(size for size in range(1, most + 1) if total % size == 0)


class Sizes:
    def __init__(self, chan, height, width, bands, taps):
        self.chan, self.height, self.width, self.bands = chan, height, width, bands
        self.side = math.isqrt(taps)
        self.margin = self.side // 2
        self.rows = height // bands
        self.wide = round_up(width + 2 * self.margin, LANES)
        self.tiles = self.wide // LANES
        self.tail = width - (self.tiles - 1) * LANES
        self.pad = round_up(chan + 1, SUBL)
        self.packed_rows = bands * self.pad
        self.tail_units = round_up(self.rows * self.tail, LANES) // LANES
        self.units = self.rows * (self.tiles - 1) + self.tail_units


def params(semantics=("arbitrary",)):
    return pltpu.CompilerParams(dimension_semantics=semantics, vmem_limit_bytes=VMEM_LIMIT)


def roll_tiles(z, tiles, shift):
    jump, low = divmod(shift % z.wide, LANES)
    count = z.tiles
    if low == 0:
        return [tiles[(j - jump) % count] for j in range(count)]
    lane = lax.broadcasted_iota(jnp.int32, tiles[0].shape, 1)
    moved = [pltpu.roll(tile, low, 1) for tile in tiles]
    return [
        jnp.where(lane < low, moved[(j - jump - 1) % count], moved[(j - jump) % count])
        for j in range(count)
    ]


def wrap_tiles(z, tiles):
    last = tiles[-1]
    lane = lax.broadcasted_iota(jnp.int32, last.shape, 1)
    ahead = pltpu.roll(tiles[0], z.tail, 1)
    behind = pltpu.roll(last, LANES - z.tail, 1)
    last = jnp.where(lane < z.tail, last, jnp.where(lane < z.tail + z.margin, ahead, behind))
    return tiles[:-1] + [last]


def row_tiles(z, value):
    tiles = [value[:, LANES * j : LANES * (j + 1)] for j in range(z.tiles - 1)]
    tail = value[:, LANES * (z.tiles - 1) :]
    zeros = jnp.zeros((value.shape[0], LANES - z.tail), F32)
    return tiles + [jnp.concatenate([tail, zeros], axis=1)]


def pack_tails(z, tails):
    lane = lax.broadcasted_iota(jnp.int32, tails[0].shape, 1)
    tiles = []
    for t in range(z.tail_units):
        begin, tile = LANES * t, None
        for row, tail in enumerate(tails):
            low = z.tail * row - begin
            if low >= LANES or low + z.tail <= 0:
                continue
            moved = pltpu.roll(tail, low % LANES, 1) if low % LANES else tail
            tile = moved if tile is None else jnp.where(lane >= low, moved, tile)
        end = z.tail * z.rows - begin
        tiles.append(jnp.where(lane < end, tile, 0.0) if end < LANES else tile)
    return tiles


def unpack_tails(z, tiles):
    lane = lax.broadcasted_iota(jnp.int32, tiles[0].shape, 1)
    tails = []
    for row in range(z.rows):
        t, low = divmod(z.tail * row, LANES)
        tail = pltpu.roll(tiles[t], LANES - low, 1) if low else tiles[t]
        if LANES - low < z.tail:
            tail = jnp.where(lane < LANES - low, tail, pltpu.roll(tiles[t + 1], LANES - low, 1))
        tails.append(jnp.where(lane < z.tail, tail, 0.0))
    return tails


def pack_rows(z, rows):
    full = z.tiles - 1
    return [row[j] for row in rows for j in range(full)] + pack_tails(z, [row[full] for row in rows])


def unpack_rows(z, tiles):
    full = z.tiles - 1
    tails = unpack_tails(z, tiles[z.rows * full :])
    return [tiles[row * full : (row + 1) * full] + [tails[row]] for row in range(z.rows)]


def packed_tiles(refs, read):
    return [
        read(ref, slice(LANES * k, LANES * (k + 1)))
        for ref in refs
        for k in range(ref.shape[-1] // LANES)
    ]


def whole(shape):
    return pl.BlockSpec(shape, lambda *_: (0,) * len(shape))


def smem():
    return pl.BlockSpec(memory_space=pltpu.SMEM)


def cost(bytes_accessed, flops=10**7):
    return pl.CostEstimate(flops=flops, bytes_accessed=bytes_accessed, transcendentals=0)


PAIR = 2
GROUP = 16


def pair_rows(z):
    return pl.BlockSpec((PAIR * z.rows, z.pad, z.width), lambda g: (g, 0, 0))


def pair_wide(z):
    return pl.BlockSpec((PAIR * z.rows, z.pad, z.wide), lambda g: (g, 0, 0))


def pair_land(z):
    return pl.BlockSpec((PAIR * z.rows, 1, z.width), lambda g: (g, 0, 0))


def pair_packed(z, cells):
    return pl.BlockSpec((PAIR * z.pad, cells), lambda g: (g, 0))


def group_rows(z):
    return pl.BlockSpec((z.height, GROUP, z.width), lambda c: (0, c, 0))


def group_wide(z):
    return pl.BlockSpec((z.height, GROUP, z.wide), lambda c: (0, c, 0))


def group_lanes(count):
    return pl.BlockSpec((count, GROUP, LANES), lambda c: (0, c, 0))


def write_pair(z, refs, bands):
    tiles = [jnp.concatenate(both, axis=0).astype(BF16) for both in zip(*bands)]
    unit = 0
    for ref in refs:
        for k in range(ref.shape[1] // LANES):
            ref[:, LANES * k : LANES * (k + 1)] = tiles[unit]
            unit += 1


def pack_out_grad(z, cells, cot, land):
    def kernel(cot_ref, land_ref, out_ref, sum_ref):
        @pl.when(pl.program_id(0) == 0)
        def _():
            sum_ref[...] = jnp.zeros_like(sum_ref)

        channel = lax.broadcasted_iota(jnp.int32, (z.pad, z.width), 0)
        total = jnp.zeros((z.pad, LANES), F32)
        bands = []
        for band in range(PAIR):
            rows = []
            for row in range(z.rows * band, z.rows * (band + 1)):
                value = cot_ref[row].astype(F32) * land_ref[row].astype(F32)
                rows.append(row_tiles(z, jnp.where(channel < z.chan, value, 0.0)))
                total = total + sum(rows[-1])
            bands.append(pack_rows(z, rows))
        sum_ref[...] += total
        write_pair(z, [out_ref], bands)

    out, sums = pl.pallas_call(
        kernel,
        grid=(z.bands // PAIR,),
        in_specs=[pair_rows(z), pair_land(z)],
        out_specs=[pair_packed(z, cells), whole((z.pad, LANES))],
        out_shape=[
            jax.ShapeDtypeStruct((z.packed_rows, cells), BF16),
            jax.ShapeDtypeStruct((z.pad, LANES), F32),
        ],
        compiler_params=params(),
        cost_estimate=cost(8 * 10**6),
    )(cot, land)
    return out, jnp.sum(sums, axis=1)[: z.chan]


def fill_rows(z, target, read, wrap):
    zeros = jnp.zeros(target.shape[1:], F32)
    for k in range(z.margin):
        target[k] = zeros
        target[z.margin + z.height + k] = zeros

    def body(h, carry):
        tiles = row_tiles(z, read(h))
        if wrap:
            tiles = wrap_tiles(z, tiles)
        for j, tile in enumerate(tiles):
            target[z.margin + h, :, LANES * j : LANES * (j + 1)] = tile
        return carry

    lax.fori_loop(0, z.height, body, 0, unroll=4)


def convolve(z, steps, at, taps_ref, source, flip, put, carry):
    span = steps + 2 * z.margin

    def body(block, carry):
        h0 = block * steps
        rows = [
            [source[h0 + m, at, LANES * j : LANES * (j + 1)] for j in range(z.tiles)]
            for m in range(span)
        ]
        sums = [None] * steps
        for b in range(z.side):
            weights = [taps_ref[z.side * a + b, at, :] for a in range(z.side)]
            for r in range(steps):
                part = None
                for a in range(z.side):
                    row = rows[r + 2 * z.margin - a] if flip else rows[r + a]
                    terms = [weights[a] * tile for tile in row]
                    part = terms if part is None else [p + t for p, t in zip(part, terms)]
                part = roll_tiles(z, part, b - z.margin if flip else z.margin - b)
                sums[r] = part if b == 0 else [s + p for s, p in zip(sums[r], part)]
        for r in range(steps):
            carry = put(h0 + r, sums[r], carry)
        return carry

    return lax.fori_loop(0, z.height // steps, body, carry)


def conv_forward(z, taps, x):
    def kernel(taps_ref, x_ref, conv_ref, sum_ref, square_ref, source):
        fill_rows(z, source, lambda h: x_ref[h].astype(F32), True)
        lane = lax.broadcasted_iota(jnp.int32, (SUBL, LANES), 1)
        for part in range(GROUP // SUBL):
            at = slice(SUBL * part, SUBL * (part + 1))

            def put(h, tiles, carry):
                for j, tile in enumerate(tiles):
                    conv_ref[h, at, LANES * j : LANES * (j + 1)] = tile
                tiles = tiles[:-1] + [jnp.where(lane < z.tail, tiles[-1], 0.0)]
                return carry[0] + sum(tiles), carry[1] + sum(t * t for t in tiles)

            @pl.when(pl.program_id(0) * GROUP + SUBL * part < z.chan)
            def _():
                zero = jnp.zeros((SUBL, LANES), F32)
                total, square = convolve(z, 4, at, taps_ref, source, False, put, (zero, zero))
                sum_ref[at, :] = total
                square_ref[at, :] = square

    lane_spec = pl.BlockSpec((GROUP, LANES), lambda c: (c, 0))
    lane_shape = jax.ShapeDtypeStruct((z.pad, LANES), F32)
    conv, total, square = pl.pallas_call(
        kernel,
        grid=(pl.cdiv(z.chan, GROUP),),
        in_specs=[group_lanes(taps.shape[0]), group_rows(z)],
        out_specs=[group_wide(z), lane_spec, lane_spec],
        out_shape=[
            jax.ShapeDtypeStruct((z.height, z.pad, z.wide), F32), lane_shape, lane_shape,
        ],
        scratch_shapes=[pltpu.VMEM((z.height + 2 * z.margin, GROUP, z.wide), F32)],
        compiler_params=params(),
        cost_estimate=cost(16 * 10**6, 10**10),
    )(taps, x)
    return conv, jnp.sum(total, axis=1)[: z.chan], jnp.sum(square, axis=1)[: z.chan]


def pack_normed(z, lengths, conv, columns):
    def kernel(columns_ref, conv_ref, *outs):
        channel = lax.broadcasted_iota(jnp.int32, (z.pad, LANES), 0)
        filler = jnp.where(channel == z.chan, 1.0, 0.0)
        mean, factor, offset = columns_ref[0], columns_ref[1], columns_ref[2]
        bands = []
        for band in range(PAIR):
            rows = []
            for row in range(z.rows * band, z.rows * (band + 1)):
                tiles = [conv_ref[row, :, LANES * j : LANES * (j + 1)] for j in range(z.tiles)]
                rows.append(
                    [
                        jnp.where(channel < z.chan, (tile - mean) * factor + offset, filler)
                        for tile in tiles
                    ]
                )
            bands.append(pack_rows(z, rows))
        write_pair(z, outs, bands)

    return pl.pallas_call(
        kernel,
        grid=(z.bands // PAIR,),
        in_specs=[whole(columns.shape), pair_wide(z)],
        out_specs=[pair_packed(z, n) for n in lengths],
        out_shape=[jax.ShapeDtypeStruct((z.packed_rows, n), BF16) for n in lengths],
        compiler_params=params(),
        cost_estimate=cost(12 * 10**6),
    )(columns, conv)


def norm_sums(z, parts, conv, columns):
    count = len(parts)

    def kernel(columns_ref, conv_ref, *rest):
        ins, (shift_ref, gain_ref) = rest[:count], rest[count:]

        @pl.when(pl.program_id(0) == 0)
        def _():
            shift_ref[...] = jnp.zeros_like(shift_ref)
            gain_ref[...] = jnp.zeros_like(gain_ref)

        mean = columns_ref[0]
        tiles = packed_tiles(ins, lambda ref, lanes: ref[:, lanes].astype(F32))
        shift = jnp.zeros((z.pad, LANES), F32)
        gain = jnp.zeros((z.pad, LANES), F32)
        for band in range(PAIR):
            rows = unpack_rows(z, [tile[z.pad * band : z.pad * (band + 1)] for tile in tiles])
            for row, grads in enumerate(rows):
                for j, grad in enumerate(grads):
                    value = conv_ref[z.rows * band + row, :, LANES * j : LANES * (j + 1)]
                    shift = shift + grad
                    gain = gain + grad * (value - mean)
        shift_ref[...] += shift
        gain_ref[...] += gain * columns_ref[1]

    lane_shape = jax.ShapeDtypeStruct((z.pad, LANES), F32)
    shift, gain = pl.pallas_call(
        kernel,
        grid=(z.bands // PAIR,),
        in_specs=[whole(columns.shape), pair_wide(z)] + [pair_packed(z, p.shape[1]) for p in parts],
        out_specs=[whole((z.pad, LANES))] * 2,
        out_shape=[lane_shape, lane_shape],
        compiler_params=params(),
        cost_estimate=cost(12 * 10**6),
    )(columns, conv, *parts)
    return jnp.sum(shift, axis=1)[: z.chan], jnp.sum(gain, axis=1)[: z.chan]


def conv_gradient(z, columns, parts, conv, x, ntaps):
    count = len(parts)
    parts = [part.reshape(z.bands, z.pad, part.shape[1]) for part in parts]
    steps = 4

    def kernel(columns_ref, conv_ref, x_ref, *rest):
        ins, (grad_ref, product_ref, grads, source) = rest[:count], rest[count:]
        mean, scale, factor, shift, gain = (columns_ref[k] for k in range(5))

        def band_body(band, carry):
            tiles = packed_tiles(ins, lambda ref, lanes: ref[band, :, lanes].astype(F32))
            for row, values in enumerate(unpack_rows(z, tiles)):
                h = band * z.rows + row
                made = []
                for j, value in enumerate(values):
                    centred = (conv_ref[h, :, LANES * j : LANES * (j + 1)] - mean) * scale
                    made.append(factor * (value - (shift + centred * gain)))
                for j, tile in enumerate(wrap_tiles(z, made)):
                    at = slice(LANES * j, LANES * (j + 1))
                    grads[h, :, at] = tile
                    grad_ref[h, :, at] = tile.astype(BF16)
            return carry

        lax.fori_loop(0, z.bands, band_body, 0)
        fill_rows(z, source, lambda h: x_ref[h].astype(F32), False)
        for part in range(GROUP // SUBL):
            at = slice(SUBL * part, SUBL * (part + 1))

            @pl.when(pl.program_id(0) * GROUP + SUBL * part < z.chan)
            def _():
                for b in range(z.side):

                    def body(block, totals):
                        h0 = block * steps
                        rows = [
                            [source[h0 + m, at, LANES * j : LANES * (j + 1)] for j in range(z.tiles)]
                            for m in range(steps + 2 * z.margin)
                        ]
                        totals = list(totals)
                        for r in range(steps):
                            moved = roll_tiles(
                                z,
                                [grads[h0 + r, at, LANES * j : LANES * (j + 1)] for j in range(z.tiles)],
                                b - z.margin,
                            )
                            for a in range(z.side):
                                for m, tile in zip(moved, rows[r + a]):
                                    totals[a] = totals[a] + m * tile
                        return tuple(totals)

                    zero = jnp.zeros((SUBL, LANES), F32)
                    totals = lax.fori_loop(0, z.height // steps, body, (zero,) * z.side)
                    for a in range(z.side):
                        product_ref[z.side * a + b, at, :] = totals[a]

    grad, products = pl.pallas_call(
        kernel,
        grid=(pl.cdiv(z.chan, GROUP),),
        in_specs=[group_lanes(5), group_wide(z), group_rows(z)]
        + [pl.BlockSpec((z.bands, GROUP, p.shape[2]), lambda c: (0, c, 0)) for p in parts],
        out_specs=[group_wide(z), group_lanes(ntaps)],
        out_shape=[
            jax.ShapeDtypeStruct((z.height, z.pad, z.wide), BF16),
            jax.ShapeDtypeStruct((ntaps, z.pad, LANES), F32),
        ],
        scratch_shapes=[
            pltpu.VMEM((z.height, GROUP, z.wide), F32),
            pltpu.VMEM((z.height + 2 * z.margin, GROUP, z.wide), F32),
        ],
        compiler_params=params(),
        cost_estimate=cost(20 * 10**6, 10**10),
    )(columns, conv, x, *parts)
    return grad, jnp.sum(products, axis=2)[:, : z.chan]


def conv_backward(z, taps, grad, cot, land):
    def kernel(taps_ref, grad_ref, cot_ref, land_ref, out_ref, source, result):
        zeros = jnp.zeros(source.shape[1:], F32)
        for k in range(z.margin):
            source[k] = zeros
            source[z.margin + z.height + k] = zeros

        def fill(h, carry):
            source[z.margin + h] = grad_ref[h].astype(F32)
            return carry

        lax.fori_loop(0, z.height, fill, 0, unroll=4)
        for part in range(GROUP // SUBL):
            at = slice(SUBL * part, SUBL * (part + 1))

            def put(h, tiles, carry):
                for j, tile in enumerate(tiles):
                    result[h, at, LANES * j : LANES * (j + 1)] = tile
                return carry

            @pl.when(pl.program_id(0) * GROUP + SUBL * part < z.chan)
            def _():
                convolve(z, 4, at, taps_ref, source, True, put, 0)

        def finish(h, carry):
            direct = cot_ref[h].astype(F32) * land_ref[h].astype(F32)
            out_ref[h] = (direct + result[h][:, : z.width]).astype(BF16)
            return carry

        lax.fori_loop(0, z.height, finish, 0, unroll=4)

    return pl.pallas_call(
        kernel,
        grid=(pl.cdiv(z.chan, GROUP),),
        in_specs=[
            group_lanes(taps.shape[0]), group_wide(z), group_rows(z),
            whole((z.height, 1, z.width)),
        ],
        out_specs=group_rows(z),
        out_shape=jax.ShapeDtypeStruct((z.height, z.chan, z.width), BF16),
        scratch_shapes=[
            pltpu.VMEM((z.height + 2 * z.margin, GROUP, z.wide), F32),
            pltpu.VMEM((z.height, GROUP, z.wide), F32),
        ],
        compiler_params=params(),
        cost_estimate=cost(16 * 10**6, 10**10),
    )(taps, grad, cot, land)


def mix_branch(z, branch, x, land):
    def kernel(x_ref, land_ref, branch_ref, out_ref):
        tiles = packed_tiles([branch_ref], lambda ref, lanes: ref[:, lanes].astype(F32))
        for band in range(PAIR):
            rows = unpack_rows(z, [tile[z.pad * band : z.pad * (band + 1)] for tile in tiles])
            for k, row in enumerate(rows):
                h = z.rows * band + k
                value = jnp.concatenate(row, axis=1)[:, : z.width]
                value = land_ref[h].astype(F32) * (x_ref[h].astype(F32) + value)
                out_ref[h] = value.astype(BF16)

    return pl.pallas_call(
        kernel,
        grid=(z.bands // PAIR,),
        in_specs=[pair_rows(z), pair_land(z), pair_packed(z, branch.shape[1])],
        out_specs=pair_rows(z),
        out_shape=jax.ShapeDtypeStruct((z.height, z.chan, z.width), BF16),
        compiler_params=params(),
        cost_estimate=cost(12 * 10**6),
    )(x, land, branch)


def gelu_parts(h):
    span = 1.0 + (0.3275911 * math.sqrt(0.5)) * jnp.abs(h)
    t = pl.reciprocal(span, approx=True)
    t = t * (2.0 - span * t)
    bell = jnp.exp2((-0.5 / math.log(2.0)) * (h * h))
    poly = t * (
        0.5 * 0.254829592
        + t
        * (
            0.5 * -0.284496736
            + t * (0.5 * 1.421413741 + t * (0.5 * -1.453152027 + t * (0.5 * 1.061405429)))
        )
    )
    tail = poly * bell
    phi = jnp.where(h >= 0, 1.0 - tail, tail)
    return h * phi, phi + h * ((1.0 / math.sqrt(2.0 * math.pi)) * bell)


def lane_block(rows, cells, part):
    return pl.BlockSpec((rows, cells), lambda *_: (0, part))


def row_step(rows, most):
    return max(n for n in range(16, most + 1, 16) if rows % n == 0)


def mlp(part, length, normed, out_grad, w_in_t, w_in, w_out, w_out_t, b_in, b_out, branch_all):
    packed, cells = normed.shape
    hidden = w_in_t.shape[0]
    block = block_of(hidden, 640)
    inner = row_step(block, 160)
    blocks = hidden // block
    pairs = block // inner // 2
    rows = row_step(packed, 208)
    outs = packed // rows

    def kernel(
        n_ref, g_ref, w_in_t_ref, w_in_ref, w_out_ref, w_out_t_ref, b_in_ref, b_out_ref, *rest
    ):
        (
            branch_ref, norm_ref, active_out, hidden_out,
            h_0, h_1, back_0, back_1, active, grads, sems,
        ) = rest[-11:]
        step = pl.program_id(0)

        def products(k, h, back):
            at = pl.ds(k * inner, inner)
            h[...] = (
                jnp.dot(w_in_t_ref[at, :], n_ref[...], preferred_element_type=F32) + b_in_ref[at, :]
            )
            back[...] = jnp.dot(w_out_ref[at, :], g_ref[:, :cells], preferred_element_type=F32)

        def gelu(k, h, back):
            at = pl.ds(pl.multiple_of(jnp.maximum(k, 0) * inner, inner), inner)
            value, slope = gelu_parts(h[...])
            active[at, :] = value.astype(BF16)
            grads[at, :] = (back[...] * slope).astype(BF16)

        @pl.when(step < blocks)
        def _():
            first = step * (2 * pairs)

            def body(i, carry):
                products(2 * i, h_0, back_0)
                gelu(first + 2 * i - 1, h_1, back_1)
                products(2 * i + 1, h_1, back_1)
                gelu(first + 2 * i, h_0, back_0)
                return carry

            lax.fori_loop(0, pairs, body, 0)

        copies = [
            pltpu.make_async_copy(active, active_out, sems.at[0]),
            pltpu.make_async_copy(grads, hidden_out, sems.at[1]),
        ]

        @pl.when(step == blocks)
        def _():
            gelu(2 * pairs * blocks - 1, h_1, back_1)
            for copy in copies:
                copy.start()

        @pl.when(step >= blocks)
        def _():
            branch = jnp.dot(w_out_t_ref[...], active[...], preferred_element_type=F32)
            branch_ref[:, :cells] = (branch + b_out_ref[...]).astype(BF16)
            norm = jnp.dot(w_in_ref[...], grads[...], preferred_element_type=F32)
            norm_ref[...] = norm.astype(BF16)

        @pl.when(step == blocks + outs - 1)
        def _():
            for copy in copies:
                copy.wait()

    def at_in(f):
        return jnp.minimum(f, blocks - 1)

    def at_out(f):
        return jnp.maximum(f - blocks, 0)

    tall_block = pl.BlockSpec((block, packed), lambda f: (at_in(f), 0))
    wide_block = pl.BlockSpec((rows, hidden), lambda f: (at_out(f), 0))
    anywhere = pl.BlockSpec(memory_space=pl.ANY)
    operands = [normed, out_grad, w_in_t, w_in, w_out, w_out_t, b_in, b_out]
    in_specs = [
        whole((packed, cells)), lane_block(packed, length, part),
        tall_block, wide_block, tall_block, wide_block,
        pl.BlockSpec((block, 1), lambda f: (at_in(f), 0)),
        pl.BlockSpec((rows, 1), lambda f: (at_out(f), 0)),
    ]
    aliases = {}
    if branch_all is not None:
        aliases = {len(operands): 0}
        operands.append(branch_all)
        in_specs.append(anywhere)
    buffer = pltpu.VMEM((inner, cells), F32)
    return pl.pallas_call(
        kernel,
        grid=(blocks + outs,),
        in_specs=in_specs,
        out_specs=[
            pl.BlockSpec((rows, length), lambda f: (at_out(f), part)),
            pl.BlockSpec((rows, cells), lambda f: (at_out(f), 0)),
            anywhere, anywhere,
        ],
        out_shape=[
            jax.ShapeDtypeStruct(out_grad.shape, BF16),
            jax.ShapeDtypeStruct((packed, cells), BF16),
            jax.ShapeDtypeStruct((hidden, cells), BF16),
            jax.ShapeDtypeStruct((hidden, cells), BF16),
        ],
        scratch_shapes=[buffer] * 4
        + [pltpu.VMEM((hidden, cells), BF16)] * 2
        + [pltpu.SemaphoreType.DMA((2,))],
        input_output_aliases=aliases,
        compiler_params=params(),
        cost_estimate=pl.CostEstimate(
            flops=8 * packed * cells * hidden, bytes_accessed=4 * 10**7, transcendentals=cells * hidden
        ),
    )(*operands)


def weight_grad(lefts, rights):
    rows, hidden = lefts[0][0].shape[0], rights[0].shape[0]
    block = block_of(hidden, 640)
    inner = row_step(rows, 208)
    arrays = []
    for array, _ in lefts:
        if not any(array is known for known in arrays):
            arrays.append(array)
    which = [next(k for k, known in enumerate(arrays) if known is array) for array, _ in lefts]

    def kernel(*refs):
        def body(m, carry):
            at = pl.ds(pl.multiple_of(m * inner, inner), inner)
            total = None
            for k, (_, start), right in zip(which, lefts, refs[len(arrays) : -1]):
                part = lax.dot_general(
                    refs[k][at, start : start + right.shape[1]], right[...],
                    (((1,), (1,)), ((), ())), preferred_element_type=F32,
                )
                total = part if total is None else total + part
            refs[-1][at, :] = total.astype(BF16)
            return carry

        lax.fori_loop(0, rows // inner, body, 0)

    cells = sum(right.shape[1] for right in rights)
    return pl.pallas_call(
        kernel,
        grid=(hidden // block,),
        in_specs=[whole(array.shape) for array in arrays]
        + [pl.BlockSpec((block, right.shape[1]), lambda f: (f, 0)) for right in rights],
        out_specs=pl.BlockSpec((rows, block), lambda f: (0, f)),
        out_shape=jax.ShapeDtypeStruct((rows, hidden), BF16),
        compiler_params=params(),
        cost_estimate=cost(24 * 10**6, 2 * rows * cells * hidden),
    )(*arrays, *rights)


def unpad_rows(z, matrix):
    groups, hidden = matrix.shape[0] // z.pad, matrix.shape[1]
    several = next(k for k in range(2, groups + 1, 2) if groups % k == 0 and k * z.chan % SUBL == 0)

    def kernel(in_ref, out_ref):
        value = in_ref[...].astype(F32)
        for k in range(several):
            out_ref[z.chan * k : z.chan * (k + 1), :] = value[z.pad * k : z.pad * k + z.chan, :]

    return pl.pallas_call(
        kernel,
        grid=(groups // several,),
        in_specs=[pl.BlockSpec((several * z.pad, hidden), lambda g: (g, 0))],
        out_specs=pl.BlockSpec((several * z.chan, hidden), lambda g: (g, 0)),
        out_shape=jax.ShapeDtypeStruct((groups * z.chan, hidden), F32),
        compiler_params=params(),
        cost_estimate=cost(16 * 10**6),
    )(matrix)


def exchange(value):
    return lax.all_to_all(value, CHAN, split_axis=0, concat_axis=0, tiled=True)


def after(value, *others):
    return lax.optimization_barrier((value, *others))[0]


def dp_sum(value):
    ways = lax.axis_size("dp")
    total = value
    for turn in range(1, ways):
        total = total + lax.ppermute(value, "dp", [(i, i ^ turn) for i in range(ways)])
    return total


def per_device(
    x_in, cotangent, land, grid_res, dw_kernel, gain, shift, res_bias, w_in, b_in, w_out, b_out
):
    samples, height, columns, chan = x_in.shape
    groups = lax.axis_size("pair") * CORES
    first = (lax.axis_index("pair") * CORES + lax.axis_index("core")) * chan
    width = chan * groups
    ntaps = dw_kernel.shape[0]
    z = Sizes(chan, height, columns, groups, ntaps)
    pixels = float(samples * lax.axis_size("dp") * height * columns)
    part = (z.units + 1) // 2 * LANES
    lengths = [part, z.units * LANES - part]
    starts = [0, part]

    def own(values, axis=0):
        return lax.dynamic_slice_in_dim(values, first, chan, axis)

    def over_lanes(rows):
        rows = jnp.pad(rows, ((0, 0), (0, z.pad - chan)))
        return jnp.broadcast_to(rows[:, :, None], rows.shape + (LANES,))

    x = jnp.transpose(x_in[0], (0, 2, 1))
    cot = jnp.transpose(cotangent[0], (0, 2, 1))
    land3 = land[0][:, None, :]

    grad_packed, part_b_out = pack_out_grad(z, sum(lengths), cot, land3)
    grad_band = exchange(grad_packed)

    taps = over_lanes(own(dw_kernel, 1).astype(F32))
    conv, total, square = conv_forward(z, taps, after(x, grad_packed))
    total, square = lax.psum((total, square), "dp")
    mean = total / pixels
    var = square / pixels - mean * mean
    scale = lax.rsqrt(var + 1e-05)
    own_gain = own(gain)
    chooser = (grid_res[:, None] == jnp.arange(2, dtype=jnp.int32)[None, :]).astype(F32)
    sample_bias = jnp.sum(chooser[0][:, None] * own(res_bias, 1), axis=0)
    affine = over_lanes(jnp.stack([mean, own_gain * scale, own(shift) + sample_bias]))
    packed = pack_normed(z, lengths, conv, affine)

    def pad_rows(matrix):
        blocks = matrix.reshape(groups, chan, matrix.shape[1])
        return jnp.pad(blocks, ((0, 0), (0, z.pad - chan), (0, 0))).reshape(
            z.packed_rows, matrix.shape[1]
        )

    w_in_p = pad_rows(after(w_in, packed[0]))
    w_in_t = w_in_p.T
    w_out_t = pad_rows(after(w_out, packed[0]).T)
    w_out_p = w_out_t.T
    weights = (w_in_t, w_in_p, w_out_p, w_out_t, b_in[:, None], pad_rows(b_out[:, None]))

    normed = [exchange(after(packed[0], grad_band))]
    normed.append(exchange(after(packed[1], normed[0], w_in_t, w_out_p)))
    branch, norm1, active1, hidden1 = mlp(0, part, normed[0], grad_band, *weights, None)
    norm_parts = [exchange(after(norm1, normed[1]))]
    branch, norm2, active2, hidden2 = mlp(1, part, normed[1], grad_band, *weights, branch)
    norm_parts.append(exchange(after(norm2, norm_parts[0])))
    g_w_out_t = weight_grad(
        [(grad_band, start) for start in starts], [active1, after(active2, norm_parts[0])]
    )
    g_w_in = weight_grad(
        [(value, 0) for value in normed], [hidden1, after(hidden2, g_w_out_t)]
    )
    branch = exchange(after(branch, norm_parts[1], g_w_in))
    everywhere = ("dp",) + CHAN
    g_w_out_t = lax.psum(g_w_out_t, everywhere)
    g_w_in = lax.psum(after(g_w_in, norm_parts[1]), everywhere)

    part_shift, part_gain = norm_sums(z, norm_parts, conv, over_lanes(jnp.stack([mean, scale])))
    small = jnp.concatenate(
        [part_shift[None], part_gain[None], chooser[0][:, None] * part_shift[None], part_b_out[None]],
        axis=0,
    )
    small = lax.psum(small, "dp")
    terms = over_lanes(
        jnp.stack([mean, scale, own_gain * scale, small[0] / pixels, small[1] / pixels])
    )
    conv_grad, g_kernel = conv_gradient(z, terms, norm_parts, conv, x, ntaps)
    g_kernel = dp_sum(g_kernel)
    x_grad = conv_backward(z, taps, conv_grad, cot, land3)
    rows = jnp.concatenate([after(g_kernel, x_grad), small], axis=0)
    gathered = lax.all_gather(rows, CHAN)
    placed = jnp.transpose(gathered, (1, 0, 2)).reshape(rows.shape[0], width)
    mixed = mix_branch(z, branch, after(x, x_grad), land3)
    g_w_out_t, g_w_in = after(g_w_out_t, mixed), after(g_w_in, mixed)

    return (
        jnp.transpose(mixed, (0, 2, 1))[None],
        jnp.transpose(x_grad, (0, 2, 1))[None],
        placed[:ntaps],
        placed[ntaps + 1],
        placed[ntaps],
        placed[ntaps + 2 : ntaps + 4],
        unpad_rows(z, g_w_in),
        g_w_in[chan].astype(F32),
        unpad_rows(z, g_w_out_t).T,
        placed[ntaps + 4],
    )


def solution(mesh):
    shape = mesh.shape
    mesh = jax.sharding.Mesh(
        mesh.devices.reshape(shape["dp"], shape["chan"] // CORES, CORES), ("dp",) + CHAN
    )
    cells = P("dp", None, None, CHAN)
    return jax.shard_map(
        per_device,
        mesh=mesh,
        in_specs=(cells, cells, P("dp", None, None), P("dp")) + (P(),) * 8,
        out_specs=(cells, cells) + (P(),) * 8,
        check_vma=False,
    )
```

time: 1410 us -> 647 us (0.46)
  other arithmetic: 409 us -> 10.4 us
  Pallas kernels: 0 us -> 357 us
  waiting for transfers between devices: 349 us -> 129 us
  matrix products: 186 us -> 0 us
  starting transfers between devices: 204 us -> 32.1 us
  local copies, waits for them, and re-layouts: 155 us -> 65.3 us
  blocking collectives: 81.3 us -> 35.8 us
    pallas_call x0 -> x13, Pallas kernels: none -> 357 us  [the longest x1 106 us: conv_gradient(): pl.pallas_call(kernel, grid=(pl.cdiv(z.chan, GROUP),), in_specs=[group_la...]
    reduce_sum x12 -> x7, other arithmetic: 283 us -> 7.26 us  [the longest x1 2.73 us: conv_gradient(): return (grad, jnp.sum(products, axis=2)[:, :z.chan])]
    all_to_all x4 -> x6, waiting for transfers between devices: 293 us -> 43.8 us  [exchange(): return lax.all_to_all(value, CHAN, split_axis=0, concat_axis=0, tiled=True)]
    dot_general x6 -> x0, matrix products: 186 us -> none  [the longest x1 77.8 us: per_device(): jnp.dot(flat_rows, w_in, preferred_element_type=jnp.float32) + b_in]
    all_to_all x4 -> x6, starting transfers between devices: 195 us -> 28.5 us  [exchange(): return lax.all_to_all(value, CHAN, split_axis=0, concat_axis=0, tiled=True)]
    convert_element_type x9 -> x2, other arithmetic: 109 us -> 1.45 us  [the longest x1 1.45 us: per_device(): g_w_in[chan].astype(F32)]
    convert_element_type x9 -> x0, local copies, waits for them, and re-layouts: 62.6 us -> none  [the longest x4 30.4 us: per_device(): cot_band.astype(jnp.float32)]
    psum x2, blocking collectives: 81.3 us -> 20 us  [the longest x1 10.1 us: per_device(): small = lax.psum(small, 'dp')]
  transfers between devices with their start and end apart: 9 -> 10, of which waited for: 4 -> 4; matrix products, arithmetic and copies ran while one was open for 15% -> 10% of each run, Pallas kernels for 0% -> 52%
where the time goes in v1:
time: 647 us; the launch traced here: 645 us
  Pallas kernels  357 us (55%)
  waiting for transfers between devices  129 us (20%)
  local copies, waits for them, and re-layouts  65.3 us (10%)
  blocking collectives  35.8 us (6%)
  starting transfers between devices  32.1 us (5%)
  between operations  14.9 us (2%)
  other arithmetic  10.4 us (2%)
    pallas_call x1, Pallas kernels, conv_gradient(): pl.pallas_call(kernel, grid=(pl.cdiv(z.chan, GROUP),), in_specs=[group_la...  106 us
    pallas_call x2, Pallas kernels, mlp(): pl.pallas_call(kernel, grid=(blocks + outs,), in_specs=in_specs, out_spec...  84.8 us
    psum x1, waiting for transfers between devices, per_device(): g_w_in = lax.psum(after(g_w_in, norm_parts[1]), everywhere)  84.3 us
    pallas_call x2, Pallas kernels, weight_grad(): pl.pallas_call(kernel, grid=(hidden // block,), in_specs=[whole(array.sha...  50.2 us
    all_to_all x6, waiting for transfers between devices, exchange(): return lax.all_to_all(value, CHAN, split_axis=0, concat_axis=0, tiled=True)  43.8 us
    pallas_call x1, Pallas kernels, conv_forward(): pl.pallas_call(kernel, grid=(pl.cdiv(z.chan, GROUP),), in_specs=[group_la...  41.4 us
    pallas_call x1, Pallas kernels, conv_backward(): pl.pallas_call(kernel, grid=(pl.cdiv(z.chan, GROUP),), in_specs=[group_la...  36.6 us
    all_to_all x6, starting transfers between devices, exchange(): return lax.all_to_all(value, CHAN, split_axis=0, concat_axis=0, tiled=True)  28.5 us
  transfers between devices with their start and end apart: 10, of which 4 were waited for; matrix products, arithmetic and copies ran while one was open for 10% of the time, Pallas kernels for 52%

profile of v1, /device:TPU:0, one launch (start us, length us, event | category | flops | bytes accessed | tf_op | source)
XLA Modules:
  0.0 644.7 jit_solution(13522951222504031955)
XLA Ops:
  7.2 1.6 broadcast_in_dim_squeeze.2.land_ref
  8.8 4.7 copy.71
  13.5 5.0 shard_map.195
  18.5 6.3 all-to-all-start
  24.8 4.7 copy.72
  29.5 0.1 constant_dynamic-slice_fusion
  29.6 2.0 broadcast_in_dim.20.taps_ref
  31.6 41.4 %shard_map.196 = (f32[48,104,384]{2,1,0:T(8,128)}, f32[104,128]{1,0:T(8,128)}, f32[104,128]{1,0:T(8,128)}) custom-call(f32[49,104,128]{2,1,0:T(8,128)} %broadcast_in_dim.20.taps_ref, bf16[48,100,360]{2,1,0:T(8,128)(2,1)} %bitcast.66), custom_call_target="tpu_custom_call" | custom-call | flops 10000000000 | bytes 16000000 | tf_op jit(solution)/shard_map/pallas_call | solution.py:276
  73.0 0.9 reduce_sum.63
  73.9 0.9 reduce_sum.64
  75.5 9.9 %all-reduce.7 = (f32[100]{0:T(128)S(1)}, f32[100]{0:T(128)S(1)}) all-reduce(f32[100]{0:T(128)S(1)} %bitcast.92, f32[100]{0:T(128)S(1)} %bitcast.93), channel_id=1, replica_groups=mesh['dp'=4,'pair'=4,'core'=2] {'dp'}, use_global_device_ids=true, to_apply=%region_1.2 | all-reduce | flops 200 | bytes 1600 | tf_op jit(solution)/shard_map/psum | solution.py:751
  85.4 0.8 multiply_reduce_fusion
  86.2 0.8 add_bitcast_fusion
  86.9 0.8 multiply_bitcast_fusion
  87.7 0.8 broadcast_in_dim.22.columns_ref
  88.5 5.9 shard_map.197
  94.4 12.2 %all-to-all-done = bf16[8,104,2176]{2,1,0:T(8,128)(2,1)} async-done(((bf16[8,104,2176]{2,1,0:T(8,128)(2,1)}), bf16[8,104,2176]{2,1,0:T(8,128)(2,1)}, u32[]{:S(2)}, u32[]{:S(2)}) %all-to-all-start) | async-done | bytes 3620896 | tf_op jit(solution)/shard_map/all_to_all | solution.py:706
  106.6 3.6 all-to-all-start.1
  110.3 5.6 reshape.78
  115.9 5.6 reshape.80
  121.5 5.4 pad.34
  126.9 2.7 pad.35
  129.6 25.8 %all-to-all-done.1 = bf16[8,104,1152]{2,1,0:T(8,128)(2,1)S(1)} async-done(((bf16[8,104,1152]{2,1,0:T(8,128)(2,1)}), bf16[8,104,1152]{2,1,0:T(8,128)(2,1)S(1)}, u32[]{:S(2)}, u32[]{:S(2)}) %all-to-all-start.1) | async-done | bytes 1916960 | tf_op jit(solution)/shard_map/all_to_all | solution.py:706
  155.4 4.5 all-to-all-start.2
  159.9 8.7 %copy.57.w_in_t_ref = bf16[3200,832]{1,0:T(8,128)(2,1)} copy(bf16[3200,832]{0,1:T(8,128)(2,1)} %bitcast.60) | data formatting | bytes 10649600 | tf_op jit(solution)/shard_map/transpose | solution.py:768
  168.6 8.7 %copy.58.w_out_ref = bf16[3200,832]{1,0:T(8,128)(2,1)} copy(bf16[3200,832]{0,1:T(8,128)(2,1)} %bitcast.63) | data formatting | bytes 10649600 | tf_op jit(solution)/shard_map/transpose | solution.py:770
  177.3 1.7 broadcast_in_dim.55.b_in_ref
  179.0 0.1 reshape_broadcast_in_dim.3
  179.1 0.9 reshape.88.b_out_ref
  180.0 45.4 %shard_map.198 = (bf16[832,2176]{1,0:T(8,128)(2,1)}, bf16[832,1152]{1,0:T(8,128)(2,1)}, bf16[3200,1152]{1,0:T(8,128)(2,1)}, bf16[3200,1152]{1,0:T(8,128)(2,1)}) custom-call(bf16[832,1152]{1,0:T(8,128)(2,1)} %bitcast.78, bf16[832,2176]{1,0:T(8,128)(2,1)} %bitcast.11.g_ref.refs_0_, bf16[3200,832]{1,0:T(8,128)(2,1)} %copy.57.w_in_t_ref, ...), custom_call_target="tpu_custom_call" | custom-call | flops 24536678400 | bytes 40000000 | tf_op jit(solution)/shard_map/pallas_call | solution.py:621
  225.5 4.8 all-to-all-start.3
  230.3 39.4 %shard_map.199 = (bf16[832,2176]{1,0:T(8,128)(2,1)}, bf16[832,1024]{1,0:T(8,128)(2,1)}, bf16[3200,1024]{1,0:T(8,128)(2,1)}, bf16[3200,1024]{1,0:T(8,128)(2,1)}) custom-call(bf16[832,1024]{1,0:T(8,128)(2,1)} %bitcast.22.n_ref.refs_1_, bf16[832,2176]{1,0:T(8,128)(2,1)} %bitcast.11.g_ref.refs_0_, ...), custom_call_target="tpu_custom_call", output_to_operand_aliasing={{0}: (8, {})} | custom-call | flops 21810380800 | bytes 40000000 | tf_op jit(solution)/shard_map/pallas_call | solution.py:621
  269.7 5.8 all-to-all-done.3.rest_0_
  275.5 4.3 all-to-all-start.4
  279.8 25.3 %shard_map.203 = bf16[832,3200]{1,0:T(8,128)(2,1)} custom-call(bf16[832,2176]{1,0:T(8,128)(2,1)} %bitcast.11.g_ref.refs_0_, bf16[3200,1152]{1,0:T(8,128)(2,1)} %get-tuple-element.68.refs_1_, bf16[3200,1024]{1,0:T(8,128)(2,1)} %get-tuple-element.70.refs_2_), custom_call_target="tpu_custom_call" | custom-call | flops 11586764800 | bytes 24000000 | tf_op jit(solution)/shard_map/pallas_call | solution.py:673
  305.1 24.9 %shard_map.204 = bf16[832,3200]{1,0:T(8,128)(2,1)} custom-call(bf16[832,1152]{1,0:T(8,128)(2,1)} %bitcast.79, bf16[832,1024]{1,0:T(8,128)(2,1)} %bitcast.22.n_ref.refs_1_, bf16[3200,1152]{1,0:T(8,128)(2,1)} %get-tuple-element.66.refs_2_, bf16[3200,1024]{1,0:T(8,128)(2,1)} %get-tuple-element.71.refs_3_), custom_call_target="tpu_custom_call" | custom-call | flops 11586764800 | bytes 24000000 | tf_op jit(solution)/shard_map/pallas_call | solution.py:673
  330.0 5.0 all-to-all-start.5
  335.1 0.7 all-reduce.11.cloned.1.call-update
  335.8 0.1 reduce_sum.68
  336.0 0.7 broadcast_in_dim.21.columns_ref
  336.7 6.1 shard_map.200
  342.8 0.9 reduce_sum.66
  343.7 0.9 reduce_sum.67
  344.7 0.1 broadcast_multiply_fusion
  344.7 10.1 %psum.37 = f32[5,100]{1,0:T(8,128)S(1)} all-reduce(f32[5,100]{1,0:T(8,128)S(1)} %pad_maximum_fusion), channel_id=1, replica_groups=mesh['dp'=4,'pair'=4,'core'=2] {'dp'}, use_global_device_ids=true, to_apply=%region_8.9 | all-reduce | flops 500 | bytes 4000 | tf_op jit(solution)/shard_map/psum | solution.py:795
  354.9 0.9 broadcast_in_dim.52.columns_ref
  355.7 106.4 %shard_map.201 = (bf16[48,104,384]{2,1,0:T(8,128)(2,1)}, f32[49,104,128]{2,1,0:T(8,128)}) custom-call(f32[5,104,128]{2,1,0:T(8,128)} %broadcast_in_dim.52.columns_ref, f32[48,104,384]{2,1,0:T(8,128)} %get-tuple-element.48.conv_ref, bf16[48,100,360]{2,1,0:T(8,128)(2,1)} %bitcast.67, bf16[8,104,1152]{2,1,0:T(8,128)(2,1)} %copy-done.4, ...), custom_call_target="tpu_custom_call" | custom-call | flops 10000000000 | bytes 20000000 | tf_op jit(solution)/shard_map/pallas_call | solution.py:414
  462.2 2.7 reduce_sum.69
  465.0 0.8 collective-permute-start.1
  465.8 2.6 collective-permute-start.2
  468.5 36.6 %shard_map.202 = bf16[48,100,360]{2,1,0:T(8,128)(2,1)} custom-call(f32[49,104,128]{2,1,0:T(8,128)} %broadcast_in_dim.20.taps_ref, bf16[48,104,384]{2,1,0:T(8,128)(2,1)} %get-tuple-element.63.grad_ref, bf16[48,100,360]{2,1,0:T(8,128)(2,1)} %bitcast.71, s32[48,1,360]{2,1,0:T(1,128)} %broadcast_in_dim_squeeze.2.land_ref), custom_call_target="tpu_custom_call" | custom-call | flops 10000000000 | bytes 16000000 | tf_op jit(solution)/shard_map/pallas_call | solution.py:465
  505.1 4.4 copy.68
  509.6 15.9 %all-gather.1 = f32[8,54,100]{2,1,0:T(8,128)S(1)} all-gather(f32[1,54,100]{2,1,0:T(8,128)S(1)} %maximum_bitcast_fusion), channel_id=2, replica_groups=mesh['dp'=4,'pair'=4,'core'=2] {'pair','core'}, dimensions={0}, use_global_device_ids=true | all-gather | bytes 194400 | tf_op jit(solution)/shard_map/all_gather | solution.py:803
  525.5 0.8 slice.60
  526.3 0.7 slice.64
  527.0 0.7 squeeze.20
  527.7 0.7 squeeze.21
  528.4 0.7 squeeze.22
  529.0 6.0 shard_map.205
  535.1 84.3 %all-reduce.11.cloned.1.call-done = (bf16[832,3200]{1,0:T(8,128)(2,1)}, bf16[832,3200]{1,0:T(8,128)(2,1)}) async-done(((bf16[832,3200]{1,0:T(8,128)(2,1)}, bf16[832,3200]{1,0:T(8,128)(2,1)}), (bf16[832,3200]{1,0:T(8,128)(2,1)}, bf16[832,3200]{1,0:T(8,128)(2,1)})) %all-reduce.11.cloned.1.call-update) | async-done | bytes 10649616 | tf_op jit(solution)/shard_map/psum | solution.py:788
  619.4 7.1 %shard_map.206 = f32[800,3200]{1,0:T(8,128)} custom-call(bf16[832,3200]{1,0:T(8,128)(2,1)} %get-tuple-element.76.in_ref), custom_call_target="tpu_custom_call" | custom-call | flops 10000000 | bytes 16000000 | tf_op jit(solution)/shard_map/pallas_call | solution.py:694
  626.5 1.5 convert_reduce_fusion
  627.9 7.6 %shard_map.207 = f32[800,3200]{1,0:T(8,128)} custom-call(bf16[832,3200]{1,0:T(8,128)(2,1)} %get-tuple-element.77.in_ref), custom_call_target="tpu_custom_call" | custom-call | flops 10000000 | bytes 16000000 | tf_op jit(solution)/shard_map/pallas_call | solution.py:694
  635.5 2.3 copy.67
  (44 shorter events, 0.4 us)
Async XLA Ops:
  7.2 22.3 %copy-start = (bf16[49,800]{1,0:T(8,128)(2,1)S(1)}, bf16[49,800]{1,0:T(8,128)(2,1)}, u32[]{:S(2)}) copy-start(bf16[49,800]{1,0:T(8,128)(2,1)} %param.16) | copy-start | bytes 235204
  18.5 88.2 %all-to-all-start = ((bf16[8,104,2176]{2,1,0:T(8,128)(2,1)}), bf16[8,104,2176]{2,1,0:T(8,128)(2,1)}, u32[]{:S(2)}, u32[]{:S(2)}) async-start(bf16[8,104,2176]{2,1,0:T(8,128)(2,1)} %bitcast.76), calls=%async_computation | async-start | bytes 7241728 | tf_op jit(solution)/shard_map/all_to_all | solution.py:706
  106.6 48.7 %all-to-all-start.1 = ((bf16[8,104,1152]{2,1,0:T(8,128)(2,1)}), bf16[8,104,1152]{2,1,0:T(8,128)(2,1)S(1)}, u32[]{:S(2)}, u32[]{:S(2)}) async-start(bf16[8,104,1152]{2,1,0:T(8,128)(2,1)} %bitcast.81), calls=%async_computation.1 | async-start | bytes 3833856 | tf_op jit(solution)/shard_map/all_to_all | solution.py:706
  121.5 5.4 copy-start.2
  155.4 13.2 %copy-start.5 = (bf16[8,104,1152]{2,1,0:T(8,128)(2,1)}, bf16[8,104,1152]{2,1,0:T(8,128)(2,1)S(1)}, u32[]{:S(2)}) copy-start(bf16[8,104,1152]{2,1,0:T(8,128)(2,1)S(1)} %all-to-all-done.1) | copy-start | bytes 5750788
  155.4 70.1 %all-to-all-start.2 = ((bf16[8,104,1024]{2,1,0:T(8,128)(2,1)}), bf16[8,104,1024]{2,1,0:T(8,128)(2,1)}, u32[]{:S(2)}, u32[]{:S(2)}) async-start(bf16[8,104,1024]{2,1,0:T(8,128)(2,1)} %bitcast.82), calls=%async_computation.2 | async-start | bytes 3407872 | tf_op jit(solution)/shard_map/all_to_all | solution.py:706
  168.6 8.7 %copy-start.7 = (f32[3200]{0:T(1024)S(1)}, f32[3200]{0:T(1024)}, u32[]{:S(2)}) copy-start(f32[3200]{0:T(1024)} %param.21) | copy-start | bytes 38404
  168.6 10.4 %copy-start.8 = (f32[800]{0:T(1024)S(1)}, f32[800]{0:T(1024)}, u32[]{:S(2)}) copy-start(f32[800]{0:T(1024)} %param.23) | copy-start | bytes 9604
  225.5 50.0 %all-to-all-start.3 = ((bf16[8,104,1152]{2,1,0:T(8,128)(2,1)}), bf16[8,104,1152]{2,1,0:T(8,128)(2,1)S(1)}, u32[]{:S(2)}, u32[]{:S(2)}) async-start(bf16[8,104,1152]{2,1,0:T(8,128)(2,1)} %bitcast.80), calls=%async_computation.3 | async-start | bytes 3833856 | tf_op jit(solution)/shard_map/all_to_all | solution.py:706
  275.5 29.6 %copy-start.4 = (bf16[8,104,1152]{2,1,0:T(8,128)(2,1)}, bf16[8,104,1152]{2,1,0:T(8,128)(2,1)S(1)}, u32[]{:S(2)}) copy-start(bf16[8,104,1152]{2,1,0:T(8,128)(2,1)S(1)} %all-to-all-done.3.rest_0_) | copy-start | bytes 5750788
  275.5 54.5 %all-to-all-start.4 = ((bf16[8,104,1024]{2,1,0:T(8,128)(2,1)}), bf16[8,104,1024]{2,1,0:T(8,128)(2,1)}, u32[]{:S(2)}, u32[]{:S(2)}) async-start(bf16[8,104,1024]{2,1,0:T(8,128)(2,1)} %bitcast.83), calls=%async_computation.4 | async-start | bytes 3407872 | tf_op jit(solution)/shard_map/all_to_all | solution.py:706
  330.0 199.0 %all-to-all-start.5 = ((bf16[8,104,2176]{2,1,0:T(8,128)(2,1)}), bf16[8,104,2176]{2,1,0:T(8,128)(2,1)}, u32[]{:S(2)}, u32[]{:S(2)}) async-start(bf16[8,104,2176]{2,1,0:T(8,128)(2,1)} %bitcast.77), calls=%async_computation.5 | async-start | bytes 7241728 | tf_op jit(solution)/shard_map/all_to_all | solution.py:706
  335.0 0.8 copy-start.6
  335.0 284.4 %all-reduce.11.cloned.1.call-start = ((), (), s32[]{:S(2)}) async-start(), calls=%async_computation.6 | async-start | bytes 21299200 | tf_op jit(solution)/shard_map/psum | solution.py:788
  464.9 44.6 %collective-permute-start = (f32[49,100]{1,0:T(8,128)S(1)}, f32[49,100]{1,0:T(8,128)S(1)}, u32[]{:S(2)}, u32[]{:S(2)}) collective-permute-start(f32[49,100]{1,0:T(8,128)S(1)} %bitcast.87), channel_id=1, source_target_pairs={{0,8},{8,0},{16,24},{24,16},{1,9},{9,1},{17,25},{25,17},{2,10},{10... | collective-permute-start | bytes 58808 | tf_op jit(solution)/shard_map/ppermute | solution.py:717
  465.0 44.6 %collective-permute-start.1 = (f32[49,100]{1,0:T(8,128)S(1)}, f32[49,100]{1,0:T(8,128)S(1)}, u32[]{:S(2)}, u32[]{:S(2)}) collective-permute-start(f32[49,100]{1,0:T(8,128)S(1)} %bitcast.88), channel_id=1, source_target_pairs={{0,16},{8,24},{16,0},{24,8},{1,17},{9,25},{17,1},{25,9},{2,18},{10... | collective-permute-start | bytes 58808 | tf_op jit(solution)/shard_map/ppermute | solution.py:717
  465.8 43.7 %collective-permute-start.2 = (f32[49,100]{1,0:T(8,128)S(1)}, f32[49,100]{1,0:T(8,128)S(1)}, u32[]{:S(2)}, u32[]{:S(2)}) collective-permute-start(f32[49,100]{1,0:T(8,128)S(1)} %bitcast.89), channel_id=1, source_target_pairs={{0,24},{8,16},{16,8},{24,0},{1,25},{9,17},{17,9},{25,1},{2,26},{10... | collective-permute-start | bytes 58808 | tf_op jit(solution)/shard_map/ppermute | solution.py:717
  627.9 7.6 %copy-start.3 = (bf16[48,100,360]{2,1,0:T(8,128)(2,1)S(1)}, bf16[48,100,360]{2,1,0:T(8,128)(2,1)}, u32[]{:S(2)}) copy-start(bf16[48,100,360]{2,1,0:T(8,128)(2,1)} %shard_map.205) | copy-start | bytes 10368004
  627.9 9.9 %copy-start.1 = (bf16[49,800]{1,0:T(8,128)(2,1)S(1)}, bf16[49,800]{1,0:T(8,128)(2,1)}, u32[]{:S(2)}) copy-start(bf16[49,800]{1,0:T(8,128)(2,1)} %param.16) | copy-start | bytes 235204
Sparse Core Ops, SparseCore 0:
  342.9 276.5 all-reduce.10
